TPU v7x, 32 devices: a whole 2x2x4 slice. The times are simulated.
32 devices in a mesh: dev: 32 (over z, y, x, core).
Axes of the slice: x: 2, y: 2, z: 4, core: 2. Of those that a mesh axis runs over, the one named last changes fastest.
Arguments:
- tokens: bfloat16 [8192, 768], P('dev'), may hold values from -6 to 6
- cotangent: bfloat16 [8192, 768], P('dev'), may hold values from -6 to 6
- starts: int32 [8192], P('dev'), may hold values from 0 to 8191, as said below
- w_qkv: float32 [1769472], P('dev'), may hold values from -0.21875 to 0.21875
- m_qkv: float32 [1769472], P('dev'), may hold values from -24 to 24
- v_qkv: float32 [1769472], P('dev'), may hold values from 1.31072 to 5.24288
- w_out: float32 [589824], P('dev'), may hold values from -1.75 to 1.75
- m_out: float32 [589824], P('dev'), may hold values from -4 to 4
- v_out: float32 [589824], P('dev'), may hold values from 0.032 to 0.128
- w_up: float32 [2359296], P('dev'), may hold values from -0.21875 to 0.21875
- m_up: float32 [2359296], P('dev'), may hold values from -32 to 32
- v_up: float32 [2359296], P('dev'), may hold values from 2.94912 to 11.79648
- w_down: float32 [2359296], P('dev'), may hold values from -0.109375 to 0.109375
- m_down: float32 [2359296], P('dev'), may hold values from -40 to 40
- v_down: float32 [2359296], P('dev'), may hold values from 3.44064 to 13.9264
- vectors: float32 [9216], P('dev'), may hold values from -0.15 to 1.3, as said below
- m_vec: float32 [9216], P('dev'), may hold values from -40 to 40
- v_vec: float32 [9216], P('dev'), may hold values from 4.096 to 16.384
Outputs:
- out_tokens: bfloat16 [8192, 768], P('dev')
- input_grad: float32 [8192, 768], P('dev')
- qkv_moment: float32 [1769472], P('dev')
- qkv_second: float32 [1769472], P('dev')
- qkv_weight: float32 [1769472], P('dev')
- out_moment: float32 [589824], P('dev')
- out_second: float32 [589824], P('dev')
- out_weight: float32 [589824], P('dev')
- up_moment: float32 [2359296], P('dev')
- up_second: float32 [2359296], P('dev')
- up_weight: float32 [2359296], P('dev')
- down_moment: float32 [2359296], P('dev')
- down_second: float32 [2359296], P('dev')
- down_weight: float32 [2359296], P('dev')
- vec_moment: float32 [9216], P('dev')
- vec_second: float32 [9216], P('dev')
- vec_weight: float32 [9216], P('dev')
Inputs may be any that keep to these rules, and one draw needn't show every extreme that they name: starts[i] is the index of the first token of the sequence that holds token i; sequences are contiguous runs of 512 to 1024 tokens, one of them exactly 1024, and only the last may be cut short by the end of the array. `vectors`: the gains (columns 0 and 5 of the table) lie in 0.7 to 1.3, all other entries (biases) in -0.15 to 0.15.
All inputs are finite; a program needn't handle non-finite values.
Results may differ from a plain program's by a relative error of at most 0.012.
The roundings to bfloat16 on the way count: a program that leaves them out, or rounds other values in their place, can miss the bound.
Values may be sent and summed in bfloat16 or wider, within the bound.
No kernel may reach another device: no remote copies, remote signals or barrier semaphores. Data moves between devices by JAX's collectives and lax.ppermute only.
A program may use at most 256 MiB of HBM per device.

v0:
```python
import jax
import jax.numpy as jnp
from jax import lax
from jax.sharding import PartitionSpec as P

D = 768
HEAD_DIM = 64
FF = 3072
SEQ_MOST = 1024
STEP = 10


NORM_EPS = 1e-05
BETA_ONE = 0.9
BETA_TWO = 0.999
ADAM_EPS = 1e-08
DECAY_RATE = 0.01
NEG_LARGE = -1e30


def shifted(x, axis, by):
    length = lax.axis_size(axis)
    pairs = [(i, i + by) for i in range(length) if 0 <= i + by < length]
    return lax.ppermute(x, axis, pairs)


def layer_norm(values, gain_vec, shift_vec):
    centre = jnp.mean(values, axis=-1, keepdims=True)
    centred = values - centre
    spread = jnp.mean(centred * centred, axis=-1, keepdims=True)
    return centred * lax.rsqrt(spread + NORM_EPS) * gain_vec + shift_vec


def smooth_act(values):
    return jax.nn.gelu(values, approximate=True)


def adamw(weight, moment, second, gradient, step_rate, decay_rate):
    moment = BETA_ONE * moment + (1.0 - BETA_ONE) * gradient
    second = BETA_TWO * second + (1.0 - BETA_TWO) * gradient * gradient
    first_hat = moment / (1.0 - BETA_ONE**STEP)
    second_hat = second / (1.0 - BETA_TWO**STEP)
    weight = weight - step_rate * (
        first_hat / (jnp.sqrt(second_hat) + ADAM_EPS) + decay_rate * weight
    )
    return (moment, second, weight)


def matrix_rates():
    return (
        2.5 * D ** (-0.5),
        2.5 * max(1, D * 16 // SEQ_MOST) ** (-0.5),
        2.5 * D ** (-0.5),
        2.5 * FF ** (-0.5),
    )


def vector_rates(entries):
    column = entries % 8
    is_gain = (entries < 8 * D) & ((column == 0) | (column == 5))
    return jnp.where(is_gain, 0.3, 0.05).astype(jnp.float32)


def split_vectors(vec_all):
    return (vec_all[: 8 * D].reshape(D, 8), vec_all[8 * D :])


def unpack(flats):
    return (
        flats[0].reshape(D, 3 * D),
        flats[1].reshape(D, D),
        flats[2].reshape(D, FF),
        flats[3].reshape(FF, D),
        flats[4].astype(jnp.float32),
    )


def outer_sum(operand_a, operand_b):
    return jnp.einsum("ti,tj->ij", operand_a, operand_b, preferred_element_type=jnp.float32)


def body(
    tokens,
    cotangent,
    starts,
    w_qkv,
    m_qkv,
    v_qkv,
    w_out,
    m_out,
    v_out,
    w_up,
    m_up,
    v_up,
    w_down,
    m_down,
    v_down,
    vectors,
    m_vec,
    v_vec,
):
    low_type = jnp.bfloat16
    full = jnp.float32
    tok_rows = tokens.shape[0]
    head_count = D // HEAD_DIM
    reach_count = (SEQ_MOST + tok_rows - 2) // tok_rows
    block_rows = min(tok_rows, 512)
    block_count = tok_rows // block_rows
    window = reach_count * tok_rows + block_rows
    near_rows = (reach_count + 1) * tok_rows
    scale = HEAD_DIM ** (-0.5)
    gathered = (
        lax.all_gather(w_qkv.astype(low_type), "dev", axis=0, tiled=True),
        lax.all_gather(w_out.astype(low_type), "dev", axis=0, tiled=True),
        lax.all_gather(w_up.astype(low_type), "dev", axis=0, tiled=True),
        lax.all_gather(w_down.astype(low_type), "dev", axis=0, tiled=True),
        lax.all_gather(vectors.astype(low_type), "dev", axis=0, tiled=True),
    )
    qkv_w, out_w, up_w, down_w, vec_all = unpack(gathered)
    vec_table, up_bias = split_vectors(vec_all)
    inputs = tokens.astype(full)
    normed = layer_norm(inputs, vec_table[:, 0], vec_table[:, 1]).astype(low_type)
    joined = jnp.dot(normed, qkv_w, preferred_element_type=full)
    query = (joined[:, :D] + vec_table[:, 2]).astype(low_type)
    local_kv = jnp.concatenate(
        [joined[:, D : 2 * D], joined[:, 2 * D :] + vec_table[:, 3]], axis=1
    ).astype(low_type)
    pieces = []
    for distance in range(reach_count, 0, -1):
        pieces.append(shifted(local_kv, "dev", distance))
    near_kv = jnp.concatenate(pieces + [local_kv], axis=0)
    base_pos = lax.axis_index("dev") * tok_rows
    query_pos = base_pos + jnp.arange(tok_rows, dtype=jnp.int32)
    key_pos = base_pos - reach_count * tok_rows + jnp.arange(near_rows, dtype=jnp.int32)

    def block_scores():
        q_block = query.reshape(block_rows, head_count, HEAD_DIM)
        k_block = near_kv[:, :D].reshape(window, head_count, HEAD_DIM)
        v_block = near_kv[:, D:].reshape(window, head_count, HEAD_DIM)
        scores = jnp.einsum("qhd,khd->hqk", q_block, k_block, preferred_element_type=full) * scale
        allowed = (key_pos[None, :] >= starts[:, None]) & (key_pos[None, :] <= query_pos[:, None])
        scores = jnp.where(allowed[None], scores, NEG_LARGE)
        return (scores, q_block, k_block, v_block)

    def forward_block(blk_index):
        scores, q_block, k_block, v_block = block_scores()
        peak = jnp.max(scores, axis=-1, keepdims=True)
        weights = jnp.exp(scores - peak)
        totals = jnp.sum(weights, axis=-1, keepdims=True)
        weights_low = (weights / totals).astype(low_type)
        blended = jnp.einsum("hqk,khd->qhd", weights_low, v_block, preferred_element_type=full)
        return (blended.reshape(block_rows, D), peak[..., 0] + jnp.log(totals[..., 0]))

    blended, log_total = lax.map(forward_block, jnp.arange(block_count, dtype=jnp.int32))
    attended = blended.reshape(tok_rows, D).astype(low_type)
    branch = jnp.dot(attended, out_w, preferred_element_type=full) + vec_table[:, 4]
    middle = inputs + branch
    normed_two = layer_norm(middle, vec_table[:, 5], vec_table[:, 6]).astype(low_type)
    hidden_pre = jnp.dot(normed_two, up_w, preferred_element_type=full) + up_bias
    hidden_low = smooth_act(hidden_pre).astype(low_type)
    result = middle + (jnp.dot(hidden_low, down_w, preferred_element_type=full) + vec_table[:, 7])
    out_tokens = result.astype(low_type)
    qkv_w, out_w, up_w, down_w, vec_all = unpack(
        (
            lax.all_gather(w_qkv.astype(low_type), "dev", axis=0, tiled=True),
            lax.all_gather(w_out.astype(low_type), "dev", axis=0, tiled=True),
            lax.all_gather(w_up.astype(low_type), "dev", axis=0, tiled=True),
            lax.all_gather(w_down.astype(low_type), "dev", axis=0, tiled=True),
            lax.all_gather(vectors.astype(low_type), "dev", axis=0, tiled=True),
        )
    )
    vec_table, up_bias = split_vectors(vec_all)
    grad_out = cotangent.astype(full)
    grad_downw = outer_sum(hidden_low, cotangent)
    grad_hidden = jnp.dot(cotangent, down_w.T, preferred_element_type=full)
    act_value, act_back = jax.vjp(smooth_act, hidden_pre)
    grad_pre = act_back(grad_hidden)[0].astype(low_type)
    grad_upw = outer_sum(normed_two, grad_pre)
    grad_normed_two = jnp.dot(grad_pre, up_w.T, preferred_element_type=full)
    norm_value, norm_two_back = jax.vjp(layer_norm, middle, vec_table[:, 5], vec_table[:, 6])
    grad_mid_norm, grad_gain_two, grad_shift_two = norm_two_back(grad_normed_two)
    grad_middle = grad_out + grad_mid_norm
    grad_branch = grad_middle.astype(low_type)
    grad_outw = outer_sum(attended, grad_branch)
    grad_attended = jnp.dot(grad_branch, out_w.T, preferred_element_type=full).astype(low_type)

    def backward_block(blk_index, carried):
        grad_query, grad_near = carried
        scores, q_block, k_block, v_block = block_scores()
        log_block = lax.dynamic_index_in_dim(log_total, blk_index, 0, keepdims=False)
        weights = jnp.exp(scores - log_block[..., None])
        grad_block = grad_attended.reshape(block_rows, head_count, HEAD_DIM)
        grad_weights = jnp.einsum("qhd,khd->hqk", grad_block, v_block, preferred_element_type=full)
        inner_sum = jnp.sum(weights * grad_weights, axis=-1, keepdims=True)
        grad_scores = (weights * (grad_weights - inner_sum) * scale).astype(low_type)
        grad_q = jnp.einsum(
            "hqk,khd->qhd", grad_scores, k_block, preferred_element_type=full
        ).reshape(block_rows, D)
        grad_k = jnp.einsum(
            "hqk,qhd->khd", grad_scores, q_block, preferred_element_type=full
        ).reshape(window, D)
        grad_v = jnp.einsum(
            "hqk,qhd->khd", weights.astype(low_type), grad_block, preferred_element_type=full
        ).reshape(window, D)
        grad_query = grad_q
        current = grad_near
        grad_near = current + jnp.concatenate([grad_k, grad_v], axis=1)
        return (grad_query, grad_near)

    grad_query, grad_near = lax.fori_loop(
        0,
        block_count,
        backward_block,
        (jnp.zeros((tok_rows, D), full), jnp.zeros((near_rows, 2 * D), full)),
    )
    own_grad = grad_near[reach_count * tok_rows :]
    for distance in range(1, reach_count + 1):
        offset = (reach_count - distance) * tok_rows
        own_grad = own_grad + shifted(grad_near[offset : offset + tok_rows], "dev", -distance)
    grad_kv_low = own_grad.astype(low_type)
    grad_q_low = grad_query.astype(low_type)
    grad_joined = jnp.concatenate([grad_q_low, grad_kv_low], axis=1)
    grad_qkvw = outer_sum(normed, grad_joined)
    grad_normed = jnp.dot(grad_joined, qkv_w.T, preferred_element_type=full)
    first_value, norm_one_back = jax.vjp(layer_norm, inputs, vec_table[:, 0], vec_table[:, 1])
    grad_in_norm, grad_gain_one, grad_shift_one = norm_one_back(grad_normed)
    input_grad = grad_middle + grad_in_norm
    vec_rows = jnp.stack(
        [
            grad_gain_one,
            grad_shift_one,
            jnp.sum(grad_q_low.astype(full), axis=0),
            jnp.sum(grad_kv_low[:, D:].astype(full), axis=0),
            jnp.sum(grad_branch.astype(full), axis=0),
            grad_gain_two,
            grad_shift_two,
            jnp.sum(grad_out, axis=0),
        ],
        axis=1,
    )
    grad_vec = jnp.concatenate([vec_rows.reshape(-1), jnp.sum(grad_pre.astype(full), axis=0)])
    reduced = (
        lax.psum_scatter(grad_qkvw.reshape(-1), "dev", scatter_dimension=0, tiled=True),
        lax.psum_scatter(grad_outw.reshape(-1), "dev", scatter_dimension=0, tiled=True),
        lax.psum_scatter(grad_upw.reshape(-1), "dev", scatter_dimension=0, tiled=True),
        lax.psum_scatter(grad_downw.reshape(-1), "dev", scatter_dimension=0, tiled=True),
        lax.psum_scatter(grad_vec, "dev", scatter_dimension=0, tiled=True),
    )
    rate_qkv, rate_out, rate_up, rate_down = matrix_rates()
    entries = lax.axis_index("dev") * vectors.shape[0] + jnp.arange(
        vectors.shape[0], dtype=jnp.int32
    )
    qkv_new = adamw(w_qkv, m_qkv, v_qkv, reduced[0], rate_qkv, DECAY_RATE)
    out_new = adamw(w_out, m_out, v_out, reduced[1], rate_out, DECAY_RATE)
    up_new = adamw(w_up, m_up, v_up, reduced[2], rate_up, DECAY_RATE)
    down_new = adamw(w_down, m_down, v_down, reduced[3], rate_down, DECAY_RATE)
    vec_new = adamw(vectors, m_vec, v_vec, reduced[4], vector_rates(entries), 0.0)
    return (
        out_tokens,
        input_grad,
        qkv_new[0],
        qkv_new[1],
        qkv_new[2],
        out_new[0],
        out_new[1],
        out_new[2],
        up_new[0],
        up_new[1],
        up_new[2],
        down_new[0],
        down_new[1],
        down_new[2],
        vec_new[0],
        vec_new[1],
        vec_new[2],
    )


def solution(mesh):
    in_specs = (
        P("dev", None),
        P("dev", None),
        P("dev"),
        P("dev"),
        P("dev"),
        P("dev"),
        P("dev"),
        P("dev"),
        P("dev"),
        P("dev"),
        P("dev"),
        P("dev"),
        P("dev"),
        P("dev"),
        P("dev"),
        P("dev"),
        P("dev"),
        P("dev"),
    )
    out_specs = (
        P("dev", None),
        P("dev", None),
        P("dev"),
        P("dev"),
        P("dev"),
        P("dev"),
        P("dev"),
        P("dev"),
        P("dev"),
        P("dev"),
        P("dev"),
        P("dev"),
        P("dev"),
        P("dev"),
        P("dev"),
        P("dev"),
        P("dev"),
    )
    return jax.shard_map(body, mesh=mesh, in_specs=in_specs, out_specs=out_specs, check_vma=False)
```

profile of v0, /device:TPU:12, one launch (start us, length us, event | category | flops | bytes accessed | tf_op | source)
XLA Modules:
  0.0 956.1 jit_solution(17843496111211954780)
XLA Ops:
  10.5 1.6 convert_element_type.120
  14.9 41.5 %all-reduce = bf16[9216]{0:T(1024)(128)(2,1)S(1)} all-reduce(bf16[9216]{0:T(1024)(128)(2,1)S(1)} %dynamic-update-slice), channel_id=1, replica_groups=mesh['dev'=32] {'dev'}, use_global_device_ids=true, to_apply=%add | all-reduce | flops 9216 | bytes 36864
  56.6 2.0 slice_reduce_fusion.2
  59.0 13.4 %all-gather.5.cloned.1.call-done = bf16[1769472]{0:T(1024)(128)(2,1)} async-done(((bf16[55296]{0:T(1024)(128)(2,1)}), bf16[1769472]{0:T(1024)(128)(2,1)}) %all-gather.5.cloned.1.call-update) | async-done | bytes 3538960 | tf_op jit(solution)/shard_map/all_gather | solution.py:113
  72.5 7.6 reshape.259
  80.1 3.2 fusion.73
  84.4 2.6 collective-permute-start
  87.0 2.9 collective-permute-start.1
  90.0 3.4 collective-permute-start.2
  93.4 2.1 collective-permute-start.3
  96.5 58.4 %all-gather.7.cloned.1.call-done = bf16[589824]{0:T(1024)(128)(2,1)} async-done(((bf16[18432]{0:T(1024)(128)(2,1)}), bf16[589824]{0:T(1024)(128)(2,1)}) %all-gather.7.cloned.1.call-update) | async-done | bytes 1179664 | tf_op jit(solution)/shard_map/all_gather | solution.py:114
  154.9 2.6 reshape.263
  162.7 2.2 fusion.86
  164.9 4.0 copy.48
  168.9 4.0 copy.50
  172.9 8.5 fusion.87
  181.3 8.1 fusion.4
  189.4 7.2 fusion.39
  198.1 24.0 %all-gather.11.cloned.1.call-done = bf16[2359296]{0:T(1024)(128)(2,1)} async-done(((bf16[73728]{0:T(1024)(128)(2,1)}), bf16[2359296]{0:T(1024)(128)(2,1)}) %all-gather.11.cloned.1.call-update) | async-done | bytes 4718608 | tf_op jit(solution)/shard_map/all_gather | solution.py:116
  222.1 9.2 reshape.265
  231.3 5.5 fusion.91
  236.8 51.1 %all-gather.9.cloned.1.call-done = bf16[2359296]{0:T(1024)(128)(2,1)} async-done(((bf16[73728]{0:T(1024)(128)(2,1)}), bf16[2359296]{0:T(1024)(128)(2,1)}) %all-gather.9.cloned.1.call-update) | async-done | bytes 4718608 | tf_op jit(solution)/shard_map/all_gather | solution.py:115
  287.9 8.2 reshape.264
  296.1 9.1 convert_reduce_fusion
  305.3 2.1 multiply_reduce_fusion.1
  311.9 9.3 fusion.92
  321.2 10.1 %fusion.6 = f32[12,64,1280]{2,1,0:T(8,128)} fusion(bf16[256,12,64]{0,2,1:T(8,128)(2,1)S(1)} %bitcast.53, f32[12,256,1280]{2,1,0:T(8,128)} %get-tuple-element.124, f32[12,256]{1,0:T(8,128)S(1)} %copy-done.22), kind=kOutput, calls=%fused_computation.18 | convolution fusion | flops 511180800 | bytes 20066304 | tf_op jit(solution)/shard_map/while/body/eval_jaxpr/hqk,qhd->khd/dot_general | solution.py:202
  331.2 33.8 %fusion.12 = f32[12,64,1280]{2,1,0:T(8,128)} fusion(bf16[256,12,64]{0,2,1:T(8,128)(2,1)S(1)} %bitcast.57, f32[12,256,1280]{2,1,0:T(8,128)} %fusion.92, f32[12,256,1280]{2,1,0:T(8,128)} %get-tuple-element.124, f32[12,256]{1,0:T(8,128)S(1)} %copy-done.22), kind=kOutput, calls=%fused_computation.22 | convolution fusion | flops 530845952 | bytes 35794944 | tf_op jit(solution)/shard_map/while/body/eval_jaxpr/hqk,qhd->khd/dot_general | solution.py:199
  365.0 5.5 fusion.31
  370.6 2.6 collective-permute-start.7
  373.2 2.5 collective-permute-start.6
  375.7 3.3 collective-permute-start.5
  379.1 3.2 collective-permute-start.4
  382.3 1.8 fusion.93
  384.1 3.3 reshape.270
  389.1 5.8 copy.53
  394.9 5.8 fusion.76
  400.7 10.9 %reshape.272 = f32[2359296]{0:T(1024)} reshape(f32[3072,768]{1,0:T(8,128)} %fusion.76) | data formatting | bytes 18874368 | tf_op jit(solution)/shard_map/reshape | solution.py:246
  411.5 33.2 %convert_reduce_fusion.5 = (f32[12,64]{1,0:T(8,128)}, bf16[12,64,256]{2,1,0:T(8,128)(2,1)}) fusion(bf16[1280,12,64]{0,2,1:T(8,128)(2,1)S(1)} %bitcast.51, f32[12,256,1280]{2,1,0:T(8,128)} %fusion.92, f32[12,256,1280]{2,1,0:T(8,128)} %get-tuple-element.124, f32[12,256]{1,0:T(8,128)} %log_add_fusion), kind=kOutput, calls=%fused_computation.83 | convolution fusion | flops 531435008 | bytes 33831936 | tf_op jit(solution)/shard_map/while/body/eval_jaxpr/hqk,khd->qhd/dot_general | solution.py:196
  444.8 3.7 fusion.30
  448.5 4.2 fusion.53
  452.7 8.1 reshape.269
  464.0 6.1 fusion.35
  476.6 90.0 %all-reduce.5 = f32[9216]{0:T(1024)S(1)} all-reduce(f32[9216]{0:T(1024)S(1)} %pad_maximum_fusion.5), channel_id=6, replica_groups=mesh['dev'=32] {'dev'}, use_global_device_ids=true, to_apply=%region_24.25.clone | all-reduce | flops 9216 | bytes 73728
  568.0 375.0 %all-reduce.9.cloned.1.call-done = (f32[1769472]{0:T(1024)}, f32[589824]{0:T(1024)}, f32[2359296]{0:T(1024)}, f32[2359296]{0:T(1024)}) async-done(((f32[1769472]{0:T(1024)}, f32[589824]{0:T(1024)}, f32[2359296]{0:T(1024)}, f32[2359296]{0:T(1024)}), (f32[1769472]{0:T(1024)}, f32[589824]{0:T(1024)}, f32[2359296]{0:T(1024)}, f32[2359296]{0:T(1024)})) %all-reduce.9.cloned.1.call-update) | async-done | bytes 28311568
  943.0 2.1 multiply_subtract_fusion.2
  945.1 1.7 multiply_subtract_fusion.3
  946.8 2.5 multiply_subtract_fusion
  (164 shorter events, 32.0 us)
Async XLA Ops:
  7.2 51.4 %copy-start = (bf16[256,768]{1,0:T(8,128)(2,1)S(1)}, bf16[256,768]{1,0:T(8,128)(2,1)}, u32[]{:S(2)}) copy-start(bf16[256,768]{1,0:T(8,128)(2,1)} %param.18) | copy-start | bytes 1179652
  7.2 65.3 %all-gather.5.cloned.1.call-start = ((), (), s32[]{:S(2)}) async-start(), calls=%async_computation | async-start | bytes 3649536 | tf_op jit(solution)/shard_map/all_gather | solution.py:113
  8.9 146.0 %all-gather.7.cloned.1.call-start = ((), (), s32[]{:S(2)}) async-start(), calls=%async_computation.1 | async-start | bytes 1216512 | tf_op jit(solution)/shard_map/all_gather | solution.py:114
  10.5 211.6 %all-gather.11.cloned.1.call-start = ((), (), s32[]{:S(2)}) async-start(), calls=%async_computation.3 | async-start | bytes 4866048 | tf_op jit(solution)/shard_map/all_gather | solution.py:116
  12.2 275.7 %all-gather.9.cloned.1.call-start = ((), (), s32[]{:S(2)}) async-start(), calls=%async_computation.2 | async-start | bytes 4866048 | tf_op jit(solution)/shard_map/all_gather | solution.py:115
  13.9 929.1 %all-reduce.9.cloned.1.call-start = ((), (), s32[]{:S(2)}) async-start(), calls=%async_computation.4 | async-start | bytes 56623104
  58.8 21.3 %copy-start.23 = (f32[256]{0:T(256)}, f32[256]{0:T(256)S(1)}, u32[]{:S(2)}) copy-start(f32[256]{0:T(256)S(1)} %broadcast_multiply_fusion.1) | copy-start | bytes 3076
  59.0 21.1 %copy-start.36 = (f32[256]{0:T(256)}, f32[256]{0:T(256)S(1)}, u32[]{:S(2)}) copy-start(f32[256]{0:T(256)S(1)} %fusion.49) | copy-start | bytes 3076
  59.0 21.1 %copy-start.25 = (f32[256]{0:T(256)}, f32[256]{0:T(256)S(1)}, u32[]{:S(2)}) copy-start(f32[256]{0:T(256)S(1)} %fusion.64) | copy-start | bytes 3076
  83.3 12.3 %copy-start.44 = (s32[256]{0:T(256)S(1)}, s32[256]{0:T(256)}, u32[]{:S(2)}) copy-start(s32[256]{0:T(256)} %param.20) | copy-start | bytes 3076
  84.4 73.3 %collective-permute-start = (bf16[256,1536]{1,0:T(8,128)(2,1)}, bf16[256,1536]{1,0:T(8,128)(2,1)}, u32[]{:S(2)}, u32[]{:S(2)}) collective-permute-start(bf16[256,1536]{1,0:T(8,128)(2,1)} %pad_maximum_fusion.2), channel_id=1, source_target_pairs={{0,4},{1,5},{2,6},{3,7},{4,8},{5,9},{6,10},{7,11},{8,12},{9,13},{1... | collective-permute-start | bytes 2359304 | tf_op jit(solution)/shard_map/ppermute | solution.py:24
  87.0 72.0 %collective-permute-start.1 = (bf16[256,1536]{1,0:T(8,128)(2,1)}, bf16[256,1536]{1,0:T(8,128)(2,1)}, u32[]{:S(2)}, u32[]{:S(2)}) collective-permute-start(bf16[256,1536]{1,0:T(8,128)(2,1)} %pad_maximum_fusion.2), channel_id=1, source_target_pairs={{0,3},{1,4},{2,5},{3,6},{4,7},{5,8},{6,9},{7,10},{8,11},{9,12},{10... | collective-permute-start | bytes 2359304 | tf_op jit(solution)/shard_map/ppermute | solution.py:24
  90.0 70.2 %collective-permute-start.2 = (bf16[256,1536]{1,0:T(8,128)(2,1)}, bf16[256,1536]{1,0:T(8,128)(2,1)}, u32[]{:S(2)}, u32[]{:S(2)}) collective-permute-start(bf16[256,1536]{1,0:T(8,128)(2,1)} %pad_maximum_fusion.2), channel_id=1, source_target_pairs={{0,2},{1,3},{2,4},{3,5},{4,6},{5,7},{6,8},{7,9},{8,10},{9,11},{10,... | collective-permute-start | bytes 2359304 | tf_op jit(solution)/shard_map/ppermute | solution.py:24
  93.4 68.0 %collective-permute-start.3 = (bf16[256,1536]{1,0:T(8,128)(2,1)}, bf16[256,1536]{1,0:T(8,128)(2,1)}, u32[]{:S(2)}, u32[]{:S(2)}) collective-permute-start(bf16[256,1536]{1,0:T(8,128)(2,1)} %pad_maximum_fusion.2), channel_id=1, source_target_pairs={{0,1},{1,2},{2,3},{3,4},{4,5},{5,6},{6,7},{7,8},{8,9},{9,10},{10,1... | collective-permute-start | bytes 2359304 | tf_op jit(solution)/shard_map/ppermute | solution.py:24
  157.7 15.2 %copy-start.11 = (bf16[256,768]{0,1:T(8,128)(2,1)}, bf16[256,768]{0,1:T(8,128)(2,1)S(1)}, u32[]{:S(2)}) copy-start(bf16[256,768]{0,1:T(8,128)(2,1)S(1)} %copy.49) | copy-start | bytes 1179652
  181.3 8.1 copy-start.1
  189.4 7.2 copy-start.29
  197.2 110.2 %copy-start.27 = (f32[256]{0:T(256)}, f32[256]{0:T(256)S(1)}, u32[]{:S(2)}) copy-start(f32[256]{0:T(256)S(1)} %broadcast_multiply_fusion) | copy-start | bytes 3076
  197.5 109.9 %copy-start.31 = (f32[256]{0:T(256)}, f32[256]{0:T(256)S(1)}, u32[]{:S(2)}) copy-start(f32[256]{0:T(256)S(1)} %fusion.65) | copy-start | bytes 3076
  198.1 33.2 %copy-start.5 = (bf16[256,768]{1,0:T(8,128)(2,1)S(1)}, bf16[256,768]{1,0:T(8,128)(2,1)}, u32[]{:S(2)}) copy-start(bf16[256,768]{1,0:T(8,128)(2,1)} %param.19) | copy-start | bytes 1179652
  236.8 59.3 %copy-start.35 = (f32[3072]{0:T(1024)S(1)}, f32[3072]{0:T(1024)}, u32[]{:S(2)}) copy-start(f32[3072]{0:T(1024)} %slice.118) | copy-start | bytes 36868
  296.1 9.1 copy-start.7
  311.8 9.3 copy-start.22
  321.2 10.1 %copy-start.12 = (bf16[256,768]{0,1:T(8,128)(2,1)S(1)}, bf16[256,768]{0,1:T(8,128)(2,1)}, u32[]{:S(2)}) copy-start(bf16[256,768]{0,1:T(8,128)(2,1)} %copy-done.11) | copy-start | bytes 1179652
  370.6 74.2 %collective-permute-start.7 = (f32[256,1536]{0,1:T(8,128)}, f32[256,1536]{0,1:T(8,128)}, u32[]{:S(2)}, u32[]{:S(2)}) collective-permute-start(f32[256,1536]{0,1:T(8,128)} %get-tuple-element.115), channel_id=1, source_target_pairs={{4,0},{5,1},{6,2},{7,3},{8,4},{9,5},{10,6},{11,7},{12,8},{13,9},{1... | collective-permute-start | bytes 4718600 | tf_op jit(solution)/shard_map/ppermute | solution.py:24
  373.2 71.6 %collective-permute-start.6 = (f32[256,1536]{0,1:T(8,128)}, f32[256,1536]{0,1:T(8,128)}, u32[]{:S(2)}, u32[]{:S(2)}) collective-permute-start(f32[256,1536]{0,1:T(8,128)} %get-tuple-element.116), channel_id=1, source_target_pairs={{3,0},{4,1},{5,2},{6,3},{7,4},{8,5},{9,6},{10,7},{11,8},{12,9},{13... | collective-permute-start | bytes 4718600 | tf_op jit(solution)/shard_map/ppermute | solution.py:24
  375.7 69.0 %collective-permute-start.5 = (f32[256,1536]{0,1:T(8,128)}, f32[256,1536]{0,1:T(8,128)}, u32[]{:S(2)}, u32[]{:S(2)}) collective-permute-start(f32[256,1536]{0,1:T(8,128)} %get-tuple-element.114), channel_id=1, source_target_pairs={{2,0},{3,1},{4,2},{5,3},{6,4},{7,5},{8,6},{9,7},{10,8},{11,9},{12,... | collective-permute-start | bytes 4718600 | tf_op jit(solution)/shard_map/ppermute | solution.py:24
  379.1 65.7 %collective-permute-start.4 = (f32[256,1536]{0,1:T(8,128)}, f32[256,1536]{0,1:T(8,128)}, u32[]{:S(2)}, u32[]{:S(2)}) collective-permute-start(f32[256,1536]{0,1:T(8,128)} %get-tuple-element.113), channel_id=1, source_target_pairs={{1,0},{2,1},{3,2},{4,3},{5,4},{6,5},{7,6},{8,7},{9,8},{10,9},{11,1... | collective-permute-start | bytes 4718600 | tf_op jit(solution)/shard_map/ppermute | solution.py:24
  384.1 3.4 copy-start.10
  384.1 3.4 copy-start.28
  384.1 3.4 copy-start.32
  389.1 5.8 copy-start.6
  400.7 10.9 %copy-start.2 = (bf16[1280,768]{0,1:T(8,128)(2,1)S(1)}, bf16[1280,768]{0,1:T(8,128)(2,1)}, u32[]{:S(2)}) copy-start(bf16[1280,768]{0,1:T(8,128)(2,1)} %copy.50) | copy-start | bytes 5898244
  444.7 3.7 copy-start.16
  444.7 3.8 copy-start.24
  444.7 3.8 copy-start.26
  460.9 3.1 copy-start.41
  464.0 6.1 copy-start.8
  470.1 3.1 copy-start.4
  470.1 3.2 copy-start.39
  471.4 471.6 %copy-start.15 = (f32[55296]{0:T(1024)S(1)}, f32[55296]{0:T(1024)}, u32[]{:S(2)}) copy-start(f32[55296]{0:T(1024)} %param.21) | copy-start | bytes 663556
  471.8 473.2 %copy-start.21 = (f32[18432]{0:T(1024)S(1)}, f32[18432]{0:T(1024)}, u32[]{:S(2)}) copy-start(f32[18432]{0:T(1024)} %param.24) | copy-start | bytes 221188
  473.3 473.5 %copy-start.13 = (f32[73728]{0:T(1024)S(1)}, f32[73728]{0:T(1024)}, u32[]{:S(2)}) copy-start(f32[73728]{0:T(1024)} %param.30) | copy-start | bytes 884740
  473.3 473.5 %copy-start.14 = (f32[73728]{0:T(1024)S(1)}, f32[73728]{0:T(1024)}, u32[]{:S(2)}) copy-start(f32[73728]{0:T(1024)} %param.27) | copy-start | bytes 884740
  473.3 473.5 %copy-start.17 = (f32[73728]{0:T(1024)S(1)}, f32[73728]{0:T(1024)}, u32[]{:S(2)}) copy-start(f32[73728]{0:T(1024)} %param.32) | copy-start | bytes 884740
  473.3 473.4 %copy-start.18 = (f32[73728]{0:T(1024)S(1)}, f32[73728]{0:T(1024)}, u32[]{:S(2)}) copy-start(f32[73728]{0:T(1024)} %param.31) | copy-start | bytes 884740
  473.3 473.4 %copy-start.19 = (f32[73728]{0:T(1024)S(1)}, f32[73728]{0:T(1024)}, u32[]{:S(2)}) copy-start(f32[73728]{0:T(1024)} %param.29) | copy-start | bytes 884740
  474.6 472.1 %copy-start.20 = (f32[73728]{0:T(1024)S(1)}, f32[73728]{0:T(1024)}, u32[]{:S(2)}) copy-start(f32[73728]{0:T(1024)} %param.28) | copy-start | bytes 884740
  (10 other events, 15.3 us)
Sparse Core Ops, SparseCore 0:
  11.5 60.9 all-gather.4
  76.0 78.9 all-gather.6
  158.4 63.6 all-gather.10
  225.4 62.4 all-gather.8
  461.1 481.8 all-reduce.8
where the time goes:
time: 965 us; the launch traced here: 956 us
  waiting for transfers between devices  522 us (54%)
  matrix products  145 us (15%)
  blocking collectives  132 us (14%)
  local copies, waits for them, and re-layouts  81.7 us (8%)
  other arithmetic  38.5 us (4%)
  starting transfers between devices  23 us (2%)
  between operations  14.8 us (2%)
    unnamed x6, waiting for transfers between devices  375 us
    unnamed x2, blocking collectives  132 us
    all_gather x1, waiting for transfers between devices, body(): lax.all_gather(w_out.astype(low_type), 'dev', axis=0, tiled=True)  58.4 us
    all_gather x1, waiting for transfers between devices, body(): lax.all_gather(w_up.astype(low_type), 'dev', axis=0, tiled=True)  51.1 us
    dot_general x1, matrix products, backward_block(): jnp.einsum('hqk,qhd->khd', grad_scores, q_block, preferred_element_type=f...  33.8 us
    dot_general x1, matrix products, backward_block(): jnp.einsum('hqk,khd->qhd', grad_scores, k_block, preferred_element_type=f...  33.2 us
    all_gather x1, waiting for transfers between devices, body(): lax.all_gather(w_down.astype(low_type), 'dev', axis=0, tiled=True)  24 us
    ppermute x8, starting transfers between devices, shifted(): return lax.ppermute(x, axis, pairs)  22.8 us
  transfers between devices with their start and end apart: 13, of which 5 were waited for; matrix products, arithmetic and copies ran while one was open for 16% of the time, Pallas kernels for 0%

commit v1 on v0

v1 whole, which is shorter than its diff:
```python
import jax
import jax.numpy as jnp
from jax import lax
from jax.sharding import PartitionSpec as P

D = 768
HEAD_DIM = 64
HEADS = D // HEAD_DIM
FF = 3072
SEQ_MOST = 1024
STEP = 10
VCOLS = 12


NORM_EPS = 1e-05
BETA_ONE = 0.9
BETA_TWO = 0.999
ADAM_EPS = 1e-08
DECAY_RATE = 0.01
NEG_LARGE = -1e30

LOW = jnp.bfloat16
FULL = jnp.float32


def layer_norm(values, gain_vec, shift_vec):
    centre = jnp.mean(values, axis=-1, keepdims=True)
    centred = values - centre
    spread = jnp.mean(centred * centred, axis=-1, keepdims=True)
    return centred * lax.rsqrt(spread + NORM_EPS) * gain_vec + shift_vec


def norm_parts(values):
    centre = jnp.mean(values, axis=-1, keepdims=True)
    centred = values - centre
    spread = jnp.mean(centred * centred, axis=-1, keepdims=True)
    inverse = lax.rsqrt(spread + NORM_EPS)
    return centred * inverse, inverse


def norm_back(grad, unit, inverse, gain_vec):
    scaled = grad * gain_vec
    along = jnp.mean(scaled * unit, axis=-1, keepdims=True)
    return inverse * (scaled - jnp.mean(scaled, axis=-1, keepdims=True) - unit * along)


def smooth_act(values):
    return jax.nn.gelu(values, approximate=True)


def adamw(weight, moment, second, gradient, step_rate, decay_rate):
    moment = BETA_ONE * moment + (1.0 - BETA_ONE) * gradient
    second = BETA_TWO * second + (1.0 - BETA_TWO) * gradient * gradient
    first_hat = moment / (1.0 - BETA_ONE**STEP)
    second_hat = second / (1.0 - BETA_TWO**STEP)
    weight = weight - step_rate * (
        first_hat / (jnp.sqrt(second_hat) + ADAM_EPS) + decay_rate * weight
    )
    return (moment, second, weight)


def matrix_rates():
    return (
        2.5 * D ** (-0.5),
        2.5 * max(1, D * 16 // SEQ_MOST) ** (-0.5),
        2.5 * D ** (-0.5),
        2.5 * FF ** (-0.5),
    )


def vector_rates(entries):
    column = entries % 8
    is_gain = (entries < 8 * D) & ((column == 0) | (column == 5))
    return jnp.where(is_gain, 0.3, 0.05).astype(jnp.float32)


def shifted(x, by):
    length = lax.axis_size("dev")
    return lax.ppermute(x, "dev", [(i, i + by) for i in range(length) if 0 <= i + by < length])


def flipped(x, mask):
    return lax.ppermute(x, "dev", [(i, i ^ mask) for i in range(lax.axis_size("dev"))])


class Index:
    def __init__(self):
        self.count = lax.axis_size("dev")
        self.bits = self.count.bit_length() - 1
        self.me = lax.axis_index("dev")
        self.top = self.bits - 2
        self.quarter = self.me >> self.top
        self.lead = (4,) + (2,) * self.top
        self.middle = tuple(range(1, self.top))

    def bit(self, b):
        return (self.me >> b) & 1

    def dim(self, b):
        return self.top - b


def ordered(bit, own, other, dim):
    flag = bit == 1
    return jnp.concatenate([jnp.where(flag, other, own), jnp.where(flag, own, other)], axis=dim)


def gather_top(ix, x):
    x = x.reshape((1,) * (ix.bits - 1) + x.shape)
    near, far, both = (flipped(x, r << ix.top) for r in (1, 2, 3))
    low_bit, high_bit = ix.quarter & 1, ix.quarter >> 1
    return ordered(high_bit, ordered(low_bit, x, near, 0), ordered(low_bit, far, both, 0), 0)


def gather_bits(ix, x, bits):
    for b in bits:
        x = ordered(ix.bit(b), x, flipped(x, 1 << b), ix.dim(b))
    return x


def joined_rows(x):
    return x.reshape(-1, x.shape[-1])


def scatter_bits(ix, x, bits):
    for b in bits:
        bit, dim = ix.bit(b), ix.dim(b)
        keep = lax.dynamic_slice_in_dim(x, bit, 1, dim)
        other = flipped(lax.dynamic_slice_in_dim(x, 1 - bit, 1, dim), 1 << b)
        x = (keep.astype(FULL) + other.astype(FULL)).astype(LOW)
    return x


def scatter_top(ix, x):
    total = lax.dynamic_slice_in_dim(x, ix.quarter, 1, 0).astype(FULL)
    others = [
        flipped(lax.dynamic_slice_in_dim(x, ix.quarter ^ r, 1, 0), r << ix.top) for r in (1, 2, 3)
    ]
    for other in others:
        total = total + other.astype(FULL)
    return total.reshape(total.shape[-2:])


def spread_rows(ix, x):
    return x.reshape(ix.lead + (x.shape[0] // ix.count, x.shape[1]))


def outer_sum(operand_a, operand_b):
    return jnp.einsum("ti,tj->ij", operand_a, operand_b, preferred_element_type=FULL).astype(LOW)


def body(
    tokens,
    cotangent,
    starts,
    w_qkv,
    m_qkv,
    v_qkv,
    w_out,
    m_out,
    v_out,
    w_up,
    m_up,
    v_up,
    w_down,
    m_down,
    v_down,
    vectors,
    m_vec,
    v_vec,
):
    ix = Index()
    rows = D // ix.count
    tok_rows = tokens.shape[0]
    reach_count = (SEQ_MOST + tok_rows - 2) // tok_rows
    near_rows = (reach_count + 1) * tok_rows
    scale = HEAD_DIM ** (-0.5)
    odd = ix.bit(0) == 1
    ahead = tuple(reversed(ix.middle))
    back = ix.middle

    assert reach_count == 4
    two_before, four_before = shifted(tokens, 2), shifted(tokens, 4)
    from_mate = flipped(
        jnp.where(
            odd,
            jnp.concatenate([two_before, four_before], axis=0),
            jnp.concatenate([tokens, two_before], axis=0),
        ),
        1,
    )
    near_tokens = jnp.concatenate(
        [four_before, from_mate[tok_rows:], two_before, from_mate[:tok_rows], tokens], axis=0
    )

    vec_piece = jnp.pad(vectors.astype(LOW).reshape(rows, VCOLS), ((0, 0), (0, 128 - VCOLS)))
    first = jnp.concatenate([w_qkv.astype(LOW).reshape(rows, 3 * D), vec_piece], axis=1)
    first = gather_top(ix, first)
    half = 3 * D // 2
    left = joined_rows(gather_bits(ix, first[..., :half], ahead + (0,)))
    right = joined_rows(gather_bits(ix, first[..., half:], back + (0,)))
    qkv_w = jnp.concatenate([left, right[:, : 3 * D - half]], axis=1)
    vec_all = right[:, 3 * D - half : 3 * D - half + VCOLS].reshape(-1).astype(FULL)

    second = jnp.concatenate(
        [w_out.astype(LOW).reshape(rows, D), w_up.astype(LOW).reshape(rows, FF)], axis=1
    )
    second = joined_rows(gather_bits(ix, gather_top(ix, second), ahead + (0,)))
    out_w, up_w = second[:, :D], second[:, D:]
    down_w = joined_rows(
        gather_bits(ix, gather_top(ix, w_down.astype(LOW).reshape(4 * rows, D)), back + (0,))
    )

    vec_table, up_bias = vec_all[: 8 * D].reshape(D, 8), vec_all[8 * D :]
    gain_one, shift_one, bias_q, bias_v, bias_o, gain_two, shift_two, bias_down = (
        vec_table[:, i] for i in range(8)
    )

    inputs = tokens.astype(FULL)
    near_unit, near_inverse = norm_parts(near_tokens.astype(FULL))
    near_normed = (near_unit * gain_one + shift_one).astype(LOW)
    normed = near_normed[near_rows - tok_rows :]
    query = (jnp.dot(normed, qkv_w[:, :D], preferred_element_type=FULL) + bias_q).astype(LOW)
    kv_bias = jnp.concatenate([jnp.zeros((D,), FULL), bias_v])
    near_kv = (jnp.dot(near_normed, qkv_w[:, D:], preferred_element_type=FULL) + kv_bias).astype(
        LOW
    )
    base_pos = ix.me * tok_rows
    query_pos = base_pos + jnp.arange(tok_rows, dtype=jnp.int32)
    key_pos = base_pos - reach_count * tok_rows + jnp.arange(near_rows, dtype=jnp.int32)
    allowed = (key_pos[None, :] >= starts[:, None]) & (key_pos[None, :] <= query_pos[:, None])
    q_heads = query.reshape(tok_rows, HEADS, HEAD_DIM)
    k_heads = near_kv[:, :D].reshape(near_rows, HEADS, HEAD_DIM)
    v_heads = near_kv[:, D:].reshape(near_rows, HEADS, HEAD_DIM)

    scores = jnp.einsum("qhd,khd->hqk", q_heads, k_heads, preferred_element_type=FULL) * scale
    scores = jnp.where(allowed[None], scores, NEG_LARGE)
    peak = jnp.max(scores, axis=-1, keepdims=True)
    weights = jnp.exp(scores - peak)
    weights = weights / jnp.sum(weights, axis=-1, keepdims=True)
    weights_low = weights.astype(LOW)
    blended = jnp.einsum("hqk,khd->qhd", weights_low, v_heads, preferred_element_type=FULL)
    attended = blended.reshape(tok_rows, D).astype(LOW)

    branch = jnp.dot(attended, out_w, preferred_element_type=FULL) + bias_o
    middle = inputs + branch
    unit_two, inverse_two = norm_parts(middle)
    normed_two = (unit_two * gain_two + shift_two).astype(LOW)
    hidden_pre = jnp.dot(normed_two, up_w, preferred_element_type=FULL) + up_bias
    hidden_low = smooth_act(hidden_pre).astype(LOW)
    result = middle + (jnp.dot(hidden_low, down_w, preferred_element_type=FULL) + bias_down)
    out_tokens = result.astype(LOW)

    grad_out = cotangent.astype(FULL)
    grad_downw = outer_sum(hidden_low, cotangent)
    sum_down = scatter_top(
        ix, scatter_bits(ix, spread_rows(ix, grad_downw), (0,) + back)
    )
    grad_hidden = jnp.dot(cotangent, down_w.T, preferred_element_type=FULL)
    act_value, act_back = jax.vjp(smooth_act, hidden_pre)
    grad_pre = act_back(grad_hidden)[0].astype(LOW)
    grad_upw = outer_sum(normed_two, grad_pre)
    grad_normed_two = jnp.dot(grad_pre, up_w.T, preferred_element_type=FULL)
    grad_gain_two = jnp.sum(grad_normed_two * unit_two, axis=0)
    grad_shift_two = jnp.sum(grad_normed_two, axis=0)
    grad_middle = grad_out + norm_back(grad_normed_two, unit_two, inverse_two, gain_two)
    grad_branch = grad_middle.astype(LOW)
    grad_outw = outer_sum(attended, grad_branch)
    sum_second = scatter_top(
        ix,
        scatter_bits(
            ix,
            spread_rows(ix, jnp.concatenate([grad_outw, grad_upw], axis=1)),
            (0,) + ahead,
        ),
    )
    grad_attended = jnp.dot(grad_branch, out_w.T, preferred_element_type=FULL).astype(LOW)

    grad_heads = grad_attended.reshape(tok_rows, HEADS, HEAD_DIM)
    grad_weights = jnp.einsum("qhd,khd->hqk", grad_heads, v_heads, preferred_element_type=FULL)
    inner_sum = jnp.sum(weights * grad_weights, axis=-1, keepdims=True)
    grad_scores = (weights * (grad_weights - inner_sum) * scale).astype(LOW)
    grad_q = jnp.einsum("hqk,khd->qhd", grad_scores, k_heads, preferred_element_type=FULL)
    grad_k = jnp.einsum("hqk,qhd->khd", grad_scores, q_heads, preferred_element_type=FULL)
    grad_v = jnp.einsum("hqk,qhd->khd", weights_low, grad_heads, preferred_element_type=FULL)
    grad_q = grad_q.reshape(tok_rows, D).astype(LOW)
    grad_kv = jnp.concatenate(
        [grad_k.reshape(near_rows, D), grad_v.reshape(near_rows, D)], axis=1
    ).astype(LOW)

    grad_near = jnp.dot(grad_kv, qkv_w[:, D:].T, preferred_element_type=FULL)
    grad_near = grad_near + jnp.pad(
        jnp.dot(grad_q, qkv_w[:, :D].T, preferred_element_type=FULL),
        ((near_rows - tok_rows, 0), (0, 0)),
    )
    grad_gain_one = jnp.sum(grad_near * near_unit, axis=0)
    grad_shift_one = jnp.sum(grad_near, axis=0)
    grad_qkvw = jnp.concatenate([outer_sum(normed, grad_q), outer_sum(near_normed, grad_kv)], axis=1)

    vec_rows = jnp.stack(
        [
            grad_gain_one,
            grad_shift_one,
            jnp.sum(grad_q.astype(FULL), axis=0),
            jnp.sum(grad_kv[:, D:].astype(FULL), axis=0),
            jnp.sum(grad_branch.astype(FULL), axis=0),
            grad_gain_two,
            grad_shift_two,
            jnp.sum(grad_out, axis=0),
        ],
        axis=1,
    )
    grad_vec = jnp.concatenate([vec_rows.reshape(-1), jnp.sum(grad_pre.astype(FULL), axis=0)])
    grad_vec = jnp.pad(grad_vec.astype(LOW).reshape(D, VCOLS), ((0, 0), (0, 128 - VCOLS)))
    sum_left = scatter_bits(ix, spread_rows(ix, grad_qkvw[:, :half]), (0,) + ahead)
    sum_right = scatter_bits(
        ix,
        spread_rows(ix, jnp.concatenate([grad_qkvw[:, half:], grad_vec], axis=1)),
        (0,) + back,
    )
    sum_first = scatter_top(ix, jnp.concatenate([sum_left, sum_right], axis=-1))

    parts = grad_near.astype(LOW).reshape(reach_count + 1, tok_rows, D)
    from_mate = flipped(jnp.concatenate([parts[3], parts[1]], axis=0), 1)
    near_mate, far_mate = from_mate[:tok_rows].astype(FULL), from_mate[tok_rows:].astype(FULL)
    own = grad_near[near_rows - tok_rows :] + jnp.where(odd, 0.0, near_mate)
    two_back = parts[2].astype(FULL) + jnp.where(odd, near_mate, far_mate)
    four_back = parts[0].astype(FULL) + jnp.where(odd, far_mate, 0.0)
    own = (
        own
        + shifted(two_back.astype(LOW), -2).astype(FULL)
        + shifted(four_back.astype(LOW), -4).astype(FULL)
    )
    unit_one = near_unit[near_rows - tok_rows :]
    inverse_one = near_inverse[near_rows - tok_rows :]
    input_grad = grad_middle + norm_back(own, unit_one, inverse_one, gain_one)

    rate_qkv, rate_out, rate_up, rate_down = matrix_rates()
    entries = ix.me * vectors.shape[0] + jnp.arange(vectors.shape[0], dtype=jnp.int32)
    g_qkv = sum_first[:, : 3 * D].reshape(-1)
    g_vec = sum_first[:, 3 * D : 3 * D + VCOLS].reshape(-1)
    g_out = sum_second[:, :D].reshape(-1)
    g_up = sum_second[:, D:].reshape(-1)
    g_down = sum_down.reshape(-1)
    qkv_new = adamw(w_qkv, m_qkv, v_qkv, g_qkv, rate_qkv, DECAY_RATE)
    out_new = adamw(w_out, m_out, v_out, g_out, rate_out, DECAY_RATE)
    up_new = adamw(w_up, m_up, v_up, g_up, rate_up, DECAY_RATE)
    down_new = adamw(w_down, m_down, v_down, g_down, rate_down, DECAY_RATE)
    vec_new = adamw(vectors, m_vec, v_vec, g_vec, vector_rates(entries), 0.0)
    return (out_tokens, input_grad) + qkv_new + out_new + up_new + down_new + vec_new


def solution(mesh):
    in_specs = (P("dev", None), P("dev", None)) + (P("dev"),) * 16
    out_specs = (P("dev", None), P("dev", None)) + (P("dev"),) * 15
    return jax.shard_map(body, mesh=mesh, in_specs=in_specs, out_specs=out_specs, check_vma=False)
```

time: 965 us -> 563 us (0.58)
  waiting for transfers between devices: 522 us -> 239 us
  blocking collectives: 132 us -> 0 us
  starting transfers between devices: 23 us -> 67.2 us
  local copies, waits for them, and re-layouts: 81.7 us -> 41.6 us
  other arithmetic: 38.5 us -> 51.2 us
  between operations: 14.8 us -> 2.7 us
    unnamed x6 -> x0, waiting for transfers between devices: 375 us -> none
    ppermute x8 -> x48, waiting for transfers between devices: 0.02 us -> 239 us  [the longest x44 222 us: flipped(): lax.ppermute(x, 'dev', [(i, i ^ mask) for i in range(lax.axis_size('dev'))])]
    all_gather x4 -> x0, waiting for transfers between devices: 147 us -> none  [the longest x1 58.4 us: body(): lax.all_gather(w_out.astype(low_type), 'dev', axis=0, tiled=True)]
    unnamed x2 -> x0, blocking collectives: 132 us -> none
    reshape x7, local copies, waits for them, and re-layouts: 50 us -> 0.49 us  [the longest x1 0.15 us: body(): w_qkv.astype(LOW).reshape(rows, 3 * D)]
    ppermute x8 -> x48, starting transfers between devices: 22.8 us -> 67.2 us  [the longest x44 53.4 us: flipped(): lax.ppermute(x, 'dev', [(i, i ^ mask) for i in range(lax.axis_size('dev'))])]
    sub x0 -> x1, matrix products: none -> 10.5 us  [body(): weights = jnp.exp(scores - peak)]
    dot_general x18 -> x20, matrix products: 145 us -> 140 us  [the longest x1 33.6 us: body(): jnp.einsum('hqk,qhd->khd', grad_scores, q_heads, preferred_element_type=F...]
  transfers between devices with their start and end apart: 13 -> 48, of which waited for: 5 -> 28; matrix products, arithmetic and copies ran while one was open for 16% -> 17% of each run, Pallas kernels for 0% -> 0%
where the time goes in v1:
time: 563 us; the launch traced here: 552 us
  waiting for transfers between devices  239 us (42%)
  matrix products  150 us (27%)
  starting transfers between devices  67.2 us (12%)
  other arithmetic  51.2 us (9%)
  local copies, waits for them, and re-layouts  41.6 us (7%)
    ppermute x44, waiting for transfers between devices, flipped(): lax.ppermute(x, 'dev', [(i, i ^ mask) for i in range(lax.axis_size('dev'))])  222 us
    ppermute x44, starting transfers between devices, flipped(): lax.ppermute(x, 'dev', [(i, i ^ mask) for i in range(lax.axis_size('dev'))])  53.4 us
    dot_general x1, matrix products, body(): jnp.einsum('hqk,qhd->khd', grad_scores, q_heads, preferred_element_type=F...  33.6 us
    dot_general x1, matrix products, body(): jnp.einsum('hqk,khd->qhd', grad_scores, k_heads, preferred_element_type=F...  32.2 us
    dot_general x5, matrix products, outer_sum(): jnp.einsum('ti,tj->ij', operand_a, operand_b, preferred_element_type=FULL)  17.7 us
    ppermute x4, waiting for transfers between devices, shifted(): lax.ppermute(x, 'dev', [(i, i + by) for i in range(length) if 0 <= i + by...  16.8 us
    ppermute x4, starting transfers between devices, shifted(): lax.ppermute(x, 'dev', [(i, i + by) for i in range(length) if 0 <= i + by...  13.7 us
    unnamed x152, local copies, waits for them, and re-layouts  12.4 us
  transfers between devices with their start and end apart: 48, of which 28 were waited for; matrix products, arithmetic and copies ran while one was open for 17% of the time, Pallas kernels for 0%

profile of v1, /device:TPU:12, one launch (start us, length us, event | category | flops | bytes accessed | tf_op | source)
XLA Modules:
  0.0 551.8 jit_solution(4723782399288546889)
XLA Ops:
  3.1 2.6 collective-permute-start.4
  14.1 3.4 collective-permute-start.1
  17.6 6.4 %collective-permute-done.3 = bf16[1,1,1,1,24,2432]{5,4,3,2,1,0:T(8,128)(2,1)S(1)} collective-permute-done((bf16[1,1,1,1,24,2432]{5,4,3,2,1,0:T(8,128)(2,1)S(1)}, bf16[1,1,1,1,24,2432]{5,4,3,2,1,0:T(8,128)(2,1)S(1)}, u32[]{:S(2)}, u32[]{:S(2)}) %collective-permute-start.3) | collective-permute-done | bytes 116768 | tf_op jit(solution)/shard_map/ppermute | solution.py:83
  23.9 4.9 collective-permute-start
  33.0 11.2 %collective-permute-done.9 = bf16[4,1,1,1,24,1152]{5,4,3,2,1,0:T(8,128)(2,1)S(1)} collective-permute-done((bf16[4,1,1,1,24,1152]{5,4,3,2,1,0:T(8,128)(2,1)S(1)}, bf16[4,1,1,1,24,1152]{5,4,3,2,1,0:T(8,128)(2,1)S(1)}, u32[]{:S(2)}, u32[]{:S(2)}) %collective-permute-start.9) | collective-permute-done | bytes 221216 | tf_op jit(solution)/shard_map/ppermute | solution.py:83
  47.4 5.3 collective-permute-done.10
  53.0 15.3 %collective-permute-done.7 = bf16[4,1,2,1,24,1280]{5,4,3,2,1,0:T(8,128)(2,1)S(1)} collective-permute-done((bf16[4,1,2,1,24,1280]{5,4,3,2,1,0:T(8,128)(2,1)S(1)}, bf16[4,1,2,1,24,1280]{5,4,3,2,1,0:T(8,128)(2,1)S(1)}, u32[]{:S(2)}, u32[]{:S(2)}) %collective-permute-start.7) | collective-permute-done | bytes 491552 | tf_op jit(solution)/shard_map/ppermute | solution.py:83
  82.9 5.3 fusion.11
  90.4 14.7 %collective-permute-done.16 = bf16[4,2,1,1,24,3840]{5,4,3,2,1,0:T(8,128)(2,1)} collective-permute-done((bf16[4,2,1,1,24,3840]{5,4,3,2,1,0:T(8,128)(2,1)}, bf16[4,2,1,1,24,3840]{5,4,3,2,1,0:T(8,128)(2,1)}, u32[]{:S(2)}, u32[]{:S(2)}) %collective-permute-start.16) | collective-permute-done | bytes 1474592 | tf_op jit(solution)/shard_map/ppermute | solution.py:83
  112.2 4.1 copy.47
  116.3 4.0 copy.45
  120.3 10.5 %fusion.109 = (f32[12,256]{1,0:T(8,128)}, f32[12,256,1280]{2,1,0:T(8,128)}) fusion(bf16[256,12,64]{0,2,1:T(8,128)(2,1)S(1)} %bitcast.108, bf16[1280,12,64]{0,2,1:T(8,128)(2,1)} %bitcast.99, pred[256,1280]{1,0:T(8,128)(4,1)} %compare_and_fusion), kind=kOutput, calls=%fused_computation.286 | convolution fusion | flops 519046400 | bytes 18427904 | tf_op jit(solution)/shard_map/sub | solution.py:239
  130.7 8.6 %fusion.49 = bf16[12,64,256]{2,1,0:T(8,128)(2,1)S(1)} fusion(bf16[1280,12,64]{0,2,1:T(8,128)(2,1)} %bitcast.85, f32[12,256,1280]{2,1,0:T(8,128)} %get-tuple-element.115, f32[12,256]{1,0:T(8,128)} %get-tuple-element.114), kind=kOutput, calls=%fused_computation.86 | convolution fusion | flops 511377408 | bytes 18100224 | tf_op jit(solution)/shard_map/hqk,khd->qhd/dot_general | solution.py:242
  150.2 4.4 collective-permute-done.42
  154.6 3.1 add_convert_fusion.1
  159.4 27.9 %collective-permute-done.43 = bf16[4,2,1,1,96,768]{5,4,3,2,1,0:T(8,128)(2,1)} collective-permute-done((bf16[4,2,1,1,96,768]{5,4,3,2,1,0:T(8,128)(2,1)}, bf16[4,2,1,1,96,768]{5,4,3,2,1,0:T(8,128)(2,1)}, u32[]{:S(2)}, u32[]{:S(2)}) %collective-permute-start.43) | collective-permute-done | bytes 1179680 | tf_op jit(solution)/shard_map/ppermute | solution.py:83
  192.5 13.0 %collective-permute-done.44 = bf16[4,1,1,1,96,768]{5,4,3,2,1,0:T(8,128)(2,1)S(1)} collective-permute-done((bf16[4,1,1,1,96,768]{5,4,3,2,1,0:T(8,128)(2,1)S(1)}, bf16[4,1,1,1,96,768]{5,4,3,2,1,0:T(8,128)(2,1)S(1)}, u32[]{:S(2)}, u32[]{:S(2)}) %collective-permute-start.44) | collective-permute-done | bytes 589856 | tf_op jit(solution)/shard_map/ppermute | solution.py:83
  206.9 9.1 %collective-permute-start.47 = (bf16[1,1,1,1,96,768]{5,4,3,2,1,0:T(8,128)(2,1)S(1)}, bf16[1,1,1,1,96,768]{5,4,3,2,1,0:T(8,128)(2,1)S(1)}, u32[]{:S(2)}, u32[]{:S(2)}) collective-permute-start(bf16[1,1,1,1,96,768]{5,4,3,2,1,0:T(8,128)(2,1)S(1)} %get-tuple-element.87), channel_id=1, source_target_pairs={{0,24},{1,25},{2,26},{3,27},{4,28},{5,29},{6,30},{7,31},{8,16},{9,... | collective-permute-start | bytes 442376 | tf_op jit(solution)/shard_map/ppermute | solution.py:83
  217.4 8.7 %collective-permute-done.47 = bf16[1,1,1,1,96,768]{5,4,3,2,1,0:T(8,128)(2,1)S(1)} collective-permute-done((bf16[1,1,1,1,96,768]{5,4,3,2,1,0:T(8,128)(2,1)S(1)}, bf16[1,1,1,1,96,768]{5,4,3,2,1,0:T(8,128)(2,1)S(1)}, u32[]{:S(2)}, u32[]{:S(2)}) %collective-permute-start.47) | collective-permute-done | bytes 147488 | tf_op jit(solution)/shard_map/ppermute | solution.py:83
  233.0 3.2 collective-permute-done.20
  236.3 5.7 %collective-permute-done.19 = bf16[1,1,1,1,96,768]{5,4,3,2,1,0:T(8,128)(2,1)S(1)} collective-permute-done((bf16[1,1,1,1,96,768]{5,4,3,2,1,0:T(8,128)(2,1)S(1)}, bf16[1,1,1,1,96,768]{5,4,3,2,1,0:T(8,128)(2,1)S(1)}, u32[]{:S(2)}, u32[]{:S(2)}) %collective-permute-start.19) | collective-permute-done | bytes 147488 | tf_op jit(solution)/shard_map/ppermute | solution.py:83
  241.9 3.6 collective-permute-done.18
  246.1 13.7 %collective-permute-done.21 = bf16[4,1,1,1,96,768]{5,4,3,2,1,0:T(8,128)(2,1)S(1)} collective-permute-done((bf16[4,1,1,1,96,768]{5,4,3,2,1,0:T(8,128)(2,1)S(1)}, bf16[4,1,1,1,96,768]{5,4,3,2,1,0:T(8,128)(2,1)S(1)}, u32[]{:S(2)}, u32[]{:S(2)}) %collective-permute-start.21) | collective-permute-done | bytes 589856 | tf_op jit(solution)/shard_map/ppermute | solution.py:83
  261.6 24.1 %collective-permute-done.22 = bf16[4,1,2,1,96,768]{5,4,3,2,1,0:T(8,128)(2,1)S(1)} collective-permute-done((bf16[4,1,2,1,96,768]{5,4,3,2,1,0:T(8,128)(2,1)S(1)}, bf16[4,1,2,1,96,768]{5,4,3,2,1,0:T(8,128)(2,1)S(1)}, u32[]{:S(2)}, u32[]{:S(2)}) %collective-permute-start.22) | collective-permute-done | bytes 1179680 | tf_op jit(solution)/shard_map/ppermute | solution.py:83
  287.5 4.9 collective-permute-done.23
  297.8 3.9 fusion.111
  306.9 3.7 convolution_convert_fusion.1
  311.5 8.5 %bitcast_reduce_fusion = (bf16[12,64]{1,0:T(8,128)(2,1)S(1)}, bf16[12,64,1280]{2,1,0:T(8,128)(2,1)}) fusion(bf16[256,12,64]{0,2,1:T(8,128)(2,1)S(1)} %bitcast.103, f32[12,256,1280]{2,1,0:T(8,128)} %get-tuple-element.115, f32[12,256]{1,0:T(8,128)S(1)} %copy-done.68), kind=kOutput, calls=%fused_computation.69 | convolution fusion | flops 513146112 | bytes 18101760 | tf_op jit(solution)/shard_map/hqk,qhd->khd/dot_general | solution.py:285
  320.0 8.9 %fusion.115 = f32[12,256,1280]{2,1,0:T(8,128)} fusion(bf16[256,12,64]{0,2,1:T(8,128)(2,1)} %bitcast.104, bf16[1280,12,64]{0,2,1:T(8,128)(2,1)S(1)} %bitcast.86), kind=kOutput, calls=%fused_computation.290 | convolution fusion | flops 503316480 | bytes 18087936 | tf_op jit(solution)/shard_map/qhd,khd->hqk/dot_general | solution.py:280
  328.9 32.2 %fusion.112 = (bf16[12,64]{1,0:T(8,128)(2,1)S(1)}, bf16[12,64,256]{2,1,0:T(8,128)(2,1)}) fusion(bf16[1280,12,64]{0,2,1:T(8,128)(2,1)S(1)} %bitcast.100, f32[12,256,1280]{2,1,0:T(8,128)} %fusion.115, f32[12,256,1280]{2,1,0:T(8,128)} %get-tuple-element.115, f32[12,256]{1,0:T(8,128)} %get-tuple-element.114), kind=kOutput, calls=%fused_computation.289 | convolution fusion | flops 531238400 | bytes 33830400 | tf_op jit(solution)/shard_map/hqk,khd->qhd/dot_general | solution.py:283
  361.1 33.6 %fusion.36 = bf16[12,64,1280]{2,1,0:T(8,128)(2,1)} fusion(bf16[256,12,64]{0,2,1:T(8,128)(2,1)} %bitcast.109, f32[12,256,1280]{2,1,0:T(8,128)} %fusion.115, f32[12,256,1280]{2,1,0:T(8,128)} %get-tuple-element.115, f32[12,256]{1,0:T(8,128)} %get-tuple-element.114), kind=kOutput, calls=%fused_computation.48 | convolution fusion | flops 531828992 | bytes 33828864 | tf_op jit(solution)/shard_map/hqk,qhd->khd/dot_general | solution.py:284
  397.2 2.6 convolution_convert_fusion.3
  402.3 3.1 pad_maximum_fusion.1
  411.5 7.5 %convolution_convert_fusion.2 = bf16[768,1536]{1,0:T(8,128)(2,1)} fusion(bf16[1280,768]{1,0:T(8,128)(2,1)} %add_convert_fusion.2, bf16[1280,768]{0,1:T(8,128)(2,1)} %bitcast.110, bf16[1280,768]{0,1:T(8,128)(2,1)} %bitcast.112), kind=kOutput, calls=%fused_computation.49 | convolution fusion | flops 3028942848 | bytes 8257536 | tf_op jit(solution)/shard_map/ti,tj->ij/dot_general | solution.py:149
  419.1 6.9 %fusion.99 = (bf16[768]{0:T(1024)(128)(2,1)S(1)}, bf16[768]{0:T(1024)(128)(2,1)S(1)}, bf16[1280,768]{1,0:T(8,128)(2,1)}, f32[1280,768]{1,0:T(8,128)}, f32[1280,768]{1,0:T(8,128)}) fusion(f32[1280]{0:T(1024)S(1)} %add_rsqrt_fusion, f32[1280]{0:T(1024)S(1)} %copy-done.41, bf16[1280,768]{1,0:T(8,128)(2,1)S(1)} %copy-done.2, f32[256,768]{1,0:T(8,128)S(1)} %copy-done.28, ...), kind=kOutput, calls=%fused_computation.282 | convolution fusion | flops 3040344576 | bytes 20067328 | tf_op jit(solution)/shard_map/dot_general | solution.py:291
  431.6 5.1 fusion.52
  438.1 3.2 collective-permute-start.25
  446.3 5.6 %collective-permute-done.25 = bf16[256,768]{1,0:T(8,128)(2,1)S(1)} collective-permute-done((bf16[256,768]{1,0:T(8,128)(2,1)S(1)}, bf16[256,768]{1,0:T(8,128)(2,1)S(1)}, u32[]{:S(2)}, u32[]{:S(2)}) %collective-permute-start.25) | collective-permute-done | bytes 393248 | tf_op jit(solution)/shard_map/ppermute | solution.py:79
  451.9 11.2 %collective-permute-done.26 = bf16[256,768]{1,0:T(8,128)(2,1)S(1)} collective-permute-done((bf16[256,768]{1,0:T(8,128)(2,1)S(1)}, bf16[256,768]{1,0:T(8,128)(2,1)S(1)}, u32[]{:S(2)}, u32[]{:S(2)}) %collective-permute-start.26) | collective-permute-done | bytes 393248 | tf_op jit(solution)/shard_map/ppermute | solution.py:79
  465.2 6.2 %collective-permute-start.29 = (bf16[4,1,1,1,24,1152]{5,4,3,2,1,0:T(8,128)(2,1)S(1)}, bf16[4,1,1,1,24,1152]{5,4,3,2,1,0:T(8,128)(2,1)S(1)}, u32[]{:S(2)}, u32[]{:S(2)}) collective-permute-start(bf16[4,1,1,1,24,1152]{5,4,3,2,1,0:T(8,128)(2,1)S(1)} %constant_dynamic-slice_fusion.15), channel_id=1, source_target_pairs={{0,2},{1,3},{2,0},{3,1},{4,6},{5,7},{6,4},{7,5},{8,10},{9,11},{10,... | collective-permute-start | bytes 663560 | tf_op jit(solution)/shard_map/ppermute | solution.py:83
  472.3 4.7 collective-permute-done.29
  480.9 3.3 collective-permute-start.35
  487.5 6.1 %collective-permute-done.35 = bf16[1,1,1,1,24,2432]{5,4,3,2,1,0:T(8,128)(2,1)S(1)} collective-permute-done((bf16[1,1,1,1,24,2432]{5,4,3,2,1,0:T(8,128)(2,1)S(1)}, bf16[1,1,1,1,24,2432]{5,4,3,2,1,0:T(8,128)(2,1)S(1)}, u32[]{:S(2)}, u32[]{:S(2)}) %collective-permute-start.35) | collective-permute-done | bytes 116768 | tf_op jit(solution)/shard_map/ppermute | solution.py:83
  493.8 19.9 %collective-permute-done.37 = bf16[4,1,2,1,24,3840]{5,4,3,2,1,0:T(8,128)(2,1)} collective-permute-done((bf16[4,1,2,1,24,3840]{5,4,3,2,1,0:T(8,128)(2,1)S(1)}, bf16[4,1,2,1,24,3840]{5,4,3,2,1,0:T(8,128)(2,1)}, u32[]{:S(2)}, u32[]{:S(2)}) %collective-permute-start.37) | collective-permute-done | bytes 1474592 | tf_op jit(solution)/shard_map/ppermute | solution.py:83
  519.3 14.7 %collective-permute-done.38 = bf16[4,1,1,1,24,3840]{5,4,3,2,1,0:T(8,128)(2,1)S(1)} collective-permute-done((bf16[4,1,1,1,24,3840]{5,4,3,2,1,0:T(8,128)(2,1)}, bf16[4,1,1,1,24,3840]{5,4,3,2,1,0:T(8,128)(2,1)S(1)}, u32[]{:S(2)}, u32[]{:S(2)}) %collective-permute-start.38) | collective-permute-done | bytes 737312 | tf_op jit(solution)/shard_map/ppermute | solution.py:83
  534.4 4.3 collective-permute-start.40
  539.3 2.6 collective-permute-done.39
  541.9 6.7 %collective-permute-done.41 = bf16[1,1,1,1,24,3840]{5,4,3,2,1,0:T(8,128)(2,1)S(1)} collective-permute-done((bf16[1,1,1,1,24,3840]{5,4,3,2,1,0:T(8,128)(2,1)S(1)}, bf16[1,1,1,1,24,3840]{5,4,3,2,1,0:T(8,128)(2,1)S(1)}, u32[]{:S(2)}, u32[]{:S(2)}) %collective-permute-start.41) | collective-permute-done | bytes 184352 | tf_op jit(solution)/shard_map/ppermute | solution.py:83
  (367 shorter events, 127.1 us)
Async XLA Ops:
  2.6 11.0 %collective-permute-start.5 = (bf16[1,1,1,1,24,2432]{5,4,3,2,1,0:T(8,128)(2,1)S(1)}, bf16[1,1,1,1,24,2432]{5,4,3,2,1,0:T(8,128)(2,1)S(1)}, u32[]{:S(2)}, u32[]{:S(2)}) collective-permute-start(bf16[1,1,1,1,24,2432]{5,4,3,2,1,0:T(8,128)(2,1)S(1)} %fusion.78), channel_id=1, source_target_pairs={{0,8},{1,9},{2,10},{3,11},{4,12},{5,13},{6,14},{7,15},{8,0},{9,1},... | collective-permute-start | bytes 350216 | tf_op jit(solution)/shard_map/ppermute | solution.py:83
  3.1 11.0 %collective-permute-start.4 = (bf16[1,1,1,1,24,2432]{5,4,3,2,1,0:T(8,128)(2,1)S(1)}, bf16[1,1,1,1,24,2432]{5,4,3,2,1,0:T(8,128)(2,1)S(1)}, u32[]{:S(2)}, u32[]{:S(2)}) collective-permute-start(bf16[1,1,1,1,24,2432]{5,4,3,2,1,0:T(8,128)(2,1)S(1)} %fusion.78), channel_id=1, source_target_pairs={{0,16},{1,17},{2,18},{3,19},{4,20},{5,21},{6,22},{7,23},{8,24},{9,... | collective-permute-start | bytes 350216 | tf_op jit(solution)/shard_map/ppermute | solution.py:83
  5.7 18.3 %collective-permute-start.3 = (bf16[1,1,1,1,24,2432]{5,4,3,2,1,0:T(8,128)(2,1)S(1)}, bf16[1,1,1,1,24,2432]{5,4,3,2,1,0:T(8,128)(2,1)S(1)}, u32[]{:S(2)}, u32[]{:S(2)}) collective-permute-start(bf16[1,1,1,1,24,2432]{5,4,3,2,1,0:T(8,128)(2,1)S(1)} %fusion.78), channel_id=1, source_target_pairs={{0,24},{1,25},{2,26},{3,27},{4,28},{5,29},{6,30},{7,31},{8,16},{9,... | collective-permute-start | bytes 350216 | tf_op jit(solution)/shard_map/ppermute | solution.py:83
  8.2 20.9 %collective-permute-start.14 = (bf16[1,1,1,1,24,3840]{5,4,3,2,1,0:T(8,128)(2,1)S(1)}, bf16[1,1,1,1,24,3840]{5,4,3,2,1,0:T(8,128)(2,1)S(1)}, u32[]{:S(2)}, u32[]{:S(2)}) collective-permute-start(bf16[1,1,1,1,24,3840]{5,4,3,2,1,0:T(8,128)(2,1)S(1)} %maximum_bitcast_fusion), channel_id=1, source_target_pairs={{0,8},{1,9},{2,10},{3,11},{4,12},{5,13},{6,14},{7,15},{8,0},{9,1},... | collective-permute-start | bytes 552968 | tf_op jit(solution)/shard_map/ppermute | solution.py:83
  9.6 19.6 %collective-permute-start.13 = (bf16[1,1,1,1,24,3840]{5,4,3,2,1,0:T(8,128)(2,1)S(1)}, bf16[1,1,1,1,24,3840]{5,4,3,2,1,0:T(8,128)(2,1)S(1)}, u32[]{:S(2)}, u32[]{:S(2)}) collective-permute-start(bf16[1,1,1,1,24,3840]{5,4,3,2,1,0:T(8,128)(2,1)S(1)} %maximum_bitcast_fusion), channel_id=1, source_target_pairs={{0,16},{1,17},{2,18},{3,19},{4,20},{5,21},{6,22},{7,23},{8,24},{9,... | collective-permute-start | bytes 552968 | tf_op jit(solution)/shard_map/ppermute | solution.py:83
  13.6 18.9 %collective-permute-start.12 = (bf16[1,1,1,1,24,3840]{5,4,3,2,1,0:T(8,128)(2,1)S(1)}, bf16[1,1,1,1,24,3840]{5,4,3,2,1,0:T(8,128)(2,1)S(1)}, u32[]{:S(2)}, u32[]{:S(2)}) collective-permute-start(bf16[1,1,1,1,24,3840]{5,4,3,2,1,0:T(8,128)(2,1)S(1)} %maximum_bitcast_fusion), channel_id=1, source_target_pairs={{0,24},{1,25},{2,26},{3,27},{4,28},{5,29},{6,30},{7,31},{8,16},{9,... | collective-permute-start | bytes 552968 | tf_op jit(solution)/shard_map/ppermute | solution.py:83
  14.1 32.9 %collective-permute-start.1 = (bf16[256,768]{1,0:T(8,128)(2,1)}, bf16[256,768]{1,0:T(8,128)(2,1)S(1)}, u32[]{:S(2)}, u32[]{:S(2)}) collective-permute-start(bf16[256,768]{1,0:T(8,128)(2,1)} %param.18), channel_id=1, source_target_pairs={{0,2},{1,3},{2,4},{3,5},{4,6},{5,7},{6,8},{7,9},{8,10},{9,11},{10,... | collective-permute-start | bytes 1179656 | tf_op jit(solution)/shard_map/ppermute | solution.py:79
  23.9 23.1 %collective-permute-start = (bf16[256,768]{1,0:T(8,128)(2,1)}, bf16[256,768]{1,0:T(8,128)(2,1)S(1)}, u32[]{:S(2)}, u32[]{:S(2)}) collective-permute-start(bf16[256,768]{1,0:T(8,128)(2,1)} %param.18), channel_id=1, source_target_pairs={{0,4},{1,5},{2,6},{3,7},{4,8},{5,9},{6,10},{7,11},{8,12},{9,13},{1... | collective-permute-start | bytes 1179656 | tf_op jit(solution)/shard_map/ppermute | solution.py:79
  29.0 15.2 %collective-permute-start.9 = (bf16[4,1,1,1,24,1152]{5,4,3,2,1,0:T(8,128)(2,1)S(1)}, bf16[4,1,1,1,24,1152]{5,4,3,2,1,0:T(8,128)(2,1)S(1)}, u32[]{:S(2)}, u32[]{:S(2)}) collective-permute-start(bf16[4,1,1,1,24,1152]{5,4,3,2,1,0:T(8,128)(2,1)S(1)} %pad_maximum_fusion.29), channel_id=1, source_target_pairs={{0,4},{1,5},{2,6},{3,7},{4,0},{5,1},{6,2},{7,3},{8,12},{9,13},{10,... | collective-permute-start | bytes 663560 | tf_op jit(solution)/shard_map/ppermute | solution.py:83
  29.2 15.2 %collective-permute-start.6 = (bf16[4,1,1,1,24,1280]{5,4,3,2,1,0:T(8,128)(2,1)S(1)}, bf16[4,1,1,1,24,1280]{5,4,3,2,1,0:T(8,128)(2,1)S(1)}, u32[]{:S(2)}, u32[]{:S(2)}) collective-permute-start(bf16[4,1,1,1,24,1280]{5,4,3,2,1,0:T(8,128)(2,1)S(1)} %fusion.74), channel_id=1, source_target_pairs={{0,2},{1,3},{2,0},{3,1},{4,6},{5,7},{6,4},{7,5},{8,10},{9,11},{10,... | collective-permute-start | bytes 737288 | tf_op jit(solution)/shard_map/ppermute | solution.py:83
  32.7 35.9 %collective-permute-start.15 = (bf16[4,1,1,1,24,3840]{5,4,3,2,1,0:T(8,128)(2,1)S(1)}, bf16[4,1,1,1,24,3840]{5,4,3,2,1,0:T(8,128)(2,1)S(1)}, u32[]{:S(2)}, u32[]{:S(2)}) collective-permute-start(bf16[4,1,1,1,24,3840]{5,4,3,2,1,0:T(8,128)(2,1)S(1)} %pad_maximum_fusion.19), channel_id=1, source_target_pairs={{0,4},{1,5},{2,6},{3,7},{4,0},{5,1},{6,2},{7,3},{8,12},{9,13},{10,... | collective-permute-start | bytes 2211848 | tf_op jit(solution)/shard_map/ppermute | solution.py:83
  44.3 8.4 %collective-permute-start.10 = (bf16[4,2,1,1,24,1152]{5,4,3,2,1,0:T(8,128)(2,1)S(1)}, bf16[4,2,1,1,24,1152]{5,4,3,2,1,0:T(8,128)(2,1)S(1)}, u32[]{:S(2)}, u32[]{:S(2)}) collective-permute-start(bf16[4,2,1,1,24,1152]{5,4,3,2,1,0:T(8,128)(2,1)S(1)} %pad_maximum_fusion.22), channel_id=1, source_target_pairs={{0,2},{1,3},{2,0},{3,1},{4,6},{5,7},{6,4},{7,5},{8,10},{9,11},{10,... | collective-permute-start | bytes 1327112 | tf_op jit(solution)/shard_map/ppermute | solution.py:83
  44.5 23.8 %collective-permute-start.7 = (bf16[4,1,2,1,24,1280]{5,4,3,2,1,0:T(8,128)(2,1)S(1)}, bf16[4,1,2,1,24,1280]{5,4,3,2,1,0:T(8,128)(2,1)S(1)}, u32[]{:S(2)}, u32[]{:S(2)}) collective-permute-start(bf16[4,1,2,1,24,1280]{5,4,3,2,1,0:T(8,128)(2,1)S(1)} %pad_maximum_fusion.21), channel_id=1, source_target_pairs={{0,4},{1,5},{2,6},{3,7},{4,0},{5,1},{6,2},{7,3},{8,12},{9,13},{10,... | collective-permute-start | bytes 1474568 | tf_op jit(solution)/shard_map/ppermute | solution.py:83
  47.3 23.3 %collective-permute-start.2 = (bf16[512,768]{1,0:T(8,128)(2,1)S(1)}, bf16[512,768]{1,0:T(8,128)(2,1)S(1)}, u32[]{:S(2)}, u32[]{:S(2)}) collective-permute-start(bf16[512,768]{1,0:T(8,128)(2,1)S(1)} %maximum_select_fusion), channel_id=1, source_target_pairs={{0,1},{1,0},{2,3},{3,2},{4,5},{5,4},{6,7},{7,6},{8,9},{9,8},{10,11... | collective-permute-start | bytes 2359304 | tf_op jit(solution)/shard_map/ppermute | solution.py:83
  52.9 19.0 %collective-permute-start.11 = (bf16[4,2,2,1,24,1152]{5,4,3,2,1,0:T(8,128)(2,1)S(1)}, bf16[4,2,2,1,24,1152]{5,4,3,2,1,0:T(8,128)(2,1)S(1)}, u32[]{:S(2)}, u32[]{:S(2)}) collective-permute-start(bf16[4,2,2,1,24,1152]{5,4,3,2,1,0:T(8,128)(2,1)S(1)} %pad_maximum_fusion.17), channel_id=1, source_target_pairs={{0,1},{1,0},{2,3},{3,2},{4,5},{5,4},{6,7},{7,6},{8,9},{9,8},{10,11... | collective-permute-start | bytes 2654216 | tf_op jit(solution)/shard_map/ppermute | solution.py:83
  68.5 5.0 collective-permute-start.8
  70.1 35.0 %collective-permute-start.16 = (bf16[4,2,1,1,24,3840]{5,4,3,2,1,0:T(8,128)(2,1)}, bf16[4,2,1,1,24,3840]{5,4,3,2,1,0:T(8,128)(2,1)}, u32[]{:S(2)}, u32[]{:S(2)}) collective-permute-start(bf16[4,2,1,1,24,3840]{5,4,3,2,1,0:T(8,128)(2,1)} %pad_maximum_fusion.12), channel_id=1, source_target_pairs={{0,2},{1,3},{2,0},{3,1},{4,6},{5,7},{6,4},{7,5},{8,10},{9,11},{10,... | collective-permute-start | bytes 4423688 | tf_op jit(solution)/shard_map/ppermute | solution.py:83
  108.6 30.8 %collective-permute-start.17 = (bf16[4,2,2,1,24,3840]{5,4,3,2,1,0:T(8,128)(2,1)}, bf16[4,2,2,1,24,3840]{5,4,3,2,1,0:T(8,128)(2,1)}, u32[]{:S(2)}, u32[]{:S(2)}) collective-permute-start(bf16[4,2,2,1,24,3840]{5,4,3,2,1,0:T(8,128)(2,1)} %pad_maximum_fusion.4), channel_id=1, source_target_pairs={{0,1},{1,0},{2,3},{3,2},{4,5},{5,4},{6,7},{7,6},{8,9},{9,8},{10,11... | collective-permute-start | bytes 8847368 | tf_op jit(solution)/shard_map/ppermute | solution.py:83
  149.9 4.7 collective-permute-start.42
  158.8 28.5 %collective-permute-start.43 = (bf16[4,2,1,1,96,768]{5,4,3,2,1,0:T(8,128)(2,1)}, bf16[4,2,1,1,96,768]{5,4,3,2,1,0:T(8,128)(2,1)}, u32[]{:S(2)}, u32[]{:S(2)}) collective-permute-start(bf16[4,2,1,1,96,768]{5,4,3,2,1,0:T(8,128)(2,1)} %constant_dynamic-slice_fusion.4), channel_id=1, source_target_pairs={{0,2},{1,3},{2,0},{3,1},{4,6},{5,7},{6,4},{7,5},{8,10},{9,11},{10,... | collective-permute-start | bytes 3538952 | tf_op jit(solution)/shard_map/ppermute | solution.py:83
  190.0 15.6 %collective-permute-start.44 = (bf16[4,1,1,1,96,768]{5,4,3,2,1,0:T(8,128)(2,1)S(1)}, bf16[4,1,1,1,96,768]{5,4,3,2,1,0:T(8,128)(2,1)S(1)}, u32[]{:S(2)}, u32[]{:S(2)}) collective-permute-start(bf16[4,1,1,1,96,768]{5,4,3,2,1,0:T(8,128)(2,1)S(1)} %constant_dynamic-slice_fusion.3), channel_id=1, source_target_pairs={{0,4},{1,5},{2,6},{3,7},{4,0},{5,1},{6,2},{7,3},{8,12},{9,13},{10,... | collective-permute-start | bytes 1769480 | tf_op jit(solution)/shard_map/ppermute | solution.py:83
  206.8 10.6 %collective-permute-start.45 = (bf16[1,1,1,1,96,768]{5,4,3,2,1,0:T(8,128)(2,1)S(1)}, bf16[1,1,1,1,96,768]{5,4,3,2,1,0:T(8,128)(2,1)S(1)}, u32[]{:S(2)}, u32[]{:S(2)}) collective-permute-start(bf16[1,1,1,1,96,768]{5,4,3,2,1,0:T(8,128)(2,1)S(1)} %get-tuple-element.86), channel_id=1, source_target_pairs={{0,8},{1,9},{2,10},{3,11},{4,12},{5,13},{6,14},{7,15},{8,0},{9,1},... | collective-permute-start | bytes 442376 | tf_op jit(solution)/shard_map/ppermute | solution.py:83
  206.9 19.2 %collective-permute-start.47 = (bf16[1,1,1,1,96,768]{5,4,3,2,1,0:T(8,128)(2,1)S(1)}, bf16[1,1,1,1,96,768]{5,4,3,2,1,0:T(8,128)(2,1)S(1)}, u32[]{:S(2)}, u32[]{:S(2)}) collective-permute-start(bf16[1,1,1,1,96,768]{5,4,3,2,1,0:T(8,128)(2,1)S(1)} %get-tuple-element.87), channel_id=1, source_target_pairs={{0,24},{1,25},{2,26},{3,27},{4,28},{5,29},{6,30},{7,31},{8,16},{9,... | collective-permute-start | bytes 442376 | tf_op jit(solution)/shard_map/ppermute | solution.py:83
  216.0 11.7 %collective-permute-start.46 = (bf16[1,1,1,1,96,768]{5,4,3,2,1,0:T(8,128)(2,1)S(1)}, bf16[1,1,1,1,96,768]{5,4,3,2,1,0:T(8,128)(2,1)S(1)}, u32[]{:S(2)}, u32[]{:S(2)}) collective-permute-start(bf16[1,1,1,1,96,768]{5,4,3,2,1,0:T(8,128)(2,1)S(1)} %get-tuple-element.88), channel_id=1, source_target_pairs={{0,16},{1,17},{2,18},{3,19},{4,20},{5,21},{6,22},{7,23},{8,24},{9,... | collective-permute-start | bytes 442376 | tf_op jit(solution)/shard_map/ppermute | solution.py:83
  229.0 7.3 %collective-permute-start.20 = (bf16[1,1,1,1,96,768]{5,4,3,2,1,0:T(8,128)(2,1)S(1)}, bf16[1,1,1,1,96,768]{5,4,3,2,1,0:T(8,128)(2,1)S(1)}, u32[]{:S(2)}, u32[]{:S(2)}) collective-permute-start(bf16[1,1,1,1,96,768]{5,4,3,2,1,0:T(8,128)(2,1)S(1)} %reshape_reshape.6), channel_id=1, source_target_pairs={{0,8},{1,9},{2,10},{3,11},{4,12},{5,13},{6,14},{7,15},{8,0},{9,1},... | collective-permute-start | bytes 442376 | tf_op jit(solution)/shard_map/ppermute | solution.py:83
  231.4 10.5 %collective-permute-start.19 = (bf16[1,1,1,1,96,768]{5,4,3,2,1,0:T(8,128)(2,1)S(1)}, bf16[1,1,1,1,96,768]{5,4,3,2,1,0:T(8,128)(2,1)S(1)}, u32[]{:S(2)}, u32[]{:S(2)}) collective-permute-start(bf16[1,1,1,1,96,768]{5,4,3,2,1,0:T(8,128)(2,1)S(1)} %reshape_reshape.6), channel_id=1, source_target_pairs={{0,16},{1,17},{2,18},{3,19},{4,20},{5,21},{6,22},{7,23},{8,24},{9,... | collective-permute-start | bytes 442376 | tf_op jit(solution)/shard_map/ppermute | solution.py:83
  232.5 13.0 %collective-permute-start.18 = (bf16[1,1,1,1,96,768]{5,4,3,2,1,0:T(8,128)(2,1)S(1)}, bf16[1,1,1,1,96,768]{5,4,3,2,1,0:T(8,128)(2,1)S(1)}, u32[]{:S(2)}, u32[]{:S(2)}) collective-permute-start(bf16[1,1,1,1,96,768]{5,4,3,2,1,0:T(8,128)(2,1)S(1)} %reshape_reshape.6), channel_id=1, source_target_pairs={{0,24},{1,25},{2,26},{3,27},{4,28},{5,29},{6,30},{7,31},{8,16},{9,... | collective-permute-start | bytes 442376 | tf_op jit(solution)/shard_map/ppermute | solution.py:83
  245.7 14.0 %collective-permute-start.21 = (bf16[4,1,1,1,96,768]{5,4,3,2,1,0:T(8,128)(2,1)S(1)}, bf16[4,1,1,1,96,768]{5,4,3,2,1,0:T(8,128)(2,1)S(1)}, u32[]{:S(2)}, u32[]{:S(2)}) collective-permute-start(bf16[4,1,1,1,96,768]{5,4,3,2,1,0:T(8,128)(2,1)S(1)} %pad_maximum_fusion.20), channel_id=1, source_target_pairs={{0,2},{1,3},{2,0},{3,1},{4,6},{5,7},{6,4},{7,5},{8,10},{9,11},{10,... | collective-permute-start | bytes 1769480 | tf_op jit(solution)/shard_map/ppermute | solution.py:83
  259.9 25.7 %collective-permute-start.22 = (bf16[4,1,2,1,96,768]{5,4,3,2,1,0:T(8,128)(2,1)S(1)}, bf16[4,1,2,1,96,768]{5,4,3,2,1,0:T(8,128)(2,1)S(1)}, u32[]{:S(2)}, u32[]{:S(2)}) collective-permute-start(bf16[4,1,2,1,96,768]{5,4,3,2,1,0:T(8,128)(2,1)S(1)} %pad_maximum_fusion.13), channel_id=1, source_target_pairs={{0,4},{1,5},{2,6},{3,7},{4,0},{5,1},{6,2},{7,3},{8,12},{9,13},{10,... | collective-permute-start | bytes 3538952 | tf_op jit(solution)/shard_map/ppermute | solution.py:83
  287.5 4.9 collective-permute-start.23
  408.8 68.2 %collective-permute-start.36 = (bf16[4,2,2,1,24,3840]{5,4,3,2,1,0:T(8,128)(2,1)}, bf16[4,2,2,1,24,3840]{5,4,3,2,1,0:T(8,128)(2,1)}, u32[]{:S(2)}, u32[]{:S(2)}) collective-permute-start(bf16[4,2,2,1,24,3840]{5,4,3,2,1,0:T(8,128)(2,1)} %constant_dynamic-slice_fusion.11), channel_id=1, source_target_pairs={{0,1},{1,0},{2,3},{3,2},{4,5},{5,4},{6,7},{7,6},{8,9},{9,8},{10,11... | collective-permute-start | bytes 8847368 | tf_op jit(solution)/shard_map/ppermute | solution.py:83
  428.3 8.4 %collective-permute-start.24 = (bf16[512,768]{1,0:T(8,128)(2,1)S(1)}, bf16[512,768]{1,0:T(8,128)(2,1)S(1)}, u32[]{:S(2)}, u32[]{:S(2)}) collective-permute-start(bf16[512,768]{1,0:T(8,128)(2,1)S(1)} %pad_maximum_fusion.18), channel_id=1, source_target_pairs={{0,1},{1,0},{2,3},{3,2},{4,5},{5,4},{6,7},{7,6},{8,9},{9,8},{10,11... | collective-permute-start | bytes 2359304 | tf_op jit(solution)/shard_map/ppermute | solution.py:83
  429.3 14.2 %collective-permute-start.27 = (bf16[4,2,2,1,24,1152]{5,4,3,2,1,0:T(8,128)(2,1)S(1)}, bf16[4,2,2,1,24,1152]{5,4,3,2,1,0:T(8,128)(2,1)S(1)}, u32[]{:S(2)}, u32[]{:S(2)}) collective-permute-start(bf16[4,2,2,1,24,1152]{5,4,3,2,1,0:T(8,128)(2,1)S(1)} %constant_dynamic-slice_fusion.17), channel_id=1, source_target_pairs={{0,1},{1,0},{2,3},{3,2},{4,5},{5,4},{6,7},{7,6},{8,9},{9,8},{10,11... | collective-permute-start | bytes 2654216 | tf_op jit(solution)/shard_map/ppermute | solution.py:83
  430.0 13.9 %collective-permute-start.30 = (bf16[4,2,2,1,24,1280]{5,4,3,2,1,0:T(8,128)(2,1)S(1)}, bf16[4,2,2,1,24,1280]{5,4,3,2,1,0:T(8,128)(2,1)S(1)}, u32[]{:S(2)}, u32[]{:S(2)}) collective-permute-start(bf16[4,2,2,1,24,1280]{5,4,3,2,1,0:T(8,128)(2,1)S(1)} %constant_dynamic-slice_fusion.14), channel_id=1, source_target_pairs={{0,1},{1,0},{2,3},{3,2},{4,5},{5,4},{6,7},{7,6},{8,9},{9,8},{10,11... | collective-permute-start | bytes 2949128 | tf_op jit(solution)/shard_map/ppermute | solution.py:83
  438.1 13.9 %collective-permute-start.25 = (bf16[256,768]{1,0:T(8,128)(2,1)S(1)}, bf16[256,768]{1,0:T(8,128)(2,1)S(1)}, u32[]{:S(2)}, u32[]{:S(2)}) collective-permute-start(bf16[256,768]{1,0:T(8,128)(2,1)S(1)} %get-tuple-element.60), channel_id=1, source_target_pairs={{2,0},{3,1},{4,2},{5,3},{6,4},{7,5},{8,6},{9,7},{10,8},{11,9},{12,... | collective-permute-start | bytes 1179656 | tf_op jit(solution)/shard_map/ppermute | solution.py:79
  441.3 21.8 %collective-permute-start.26 = (bf16[256,768]{1,0:T(8,128)(2,1)S(1)}, bf16[256,768]{1,0:T(8,128)(2,1)S(1)}, u32[]{:S(2)}, u32[]{:S(2)}) collective-permute-start(bf16[256,768]{1,0:T(8,128)(2,1)S(1)} %get-tuple-element.61), channel_id=1, source_target_pairs={{4,0},{5,1},{6,2},{7,3},{8,4},{9,5},{10,6},{11,7},{12,8},{13,9},{1... | collective-permute-start | bytes 1179656 | tf_op jit(solution)/shard_map/ppermute | solution.py:79
  443.8 21.2 %collective-permute-start.28 = (bf16[4,1,2,1,24,1152]{5,4,3,2,1,0:T(8,128)(2,1)S(1)}, bf16[4,1,2,1,24,1152]{5,4,3,2,1,0:T(8,128)(2,1)S(1)}, u32[]{:S(2)}, u32[]{:S(2)}) collective-permute-start(bf16[4,1,2,1,24,1152]{5,4,3,2,1,0:T(8,128)(2,1)S(1)} %constant_dynamic-slice_fusion.16), channel_id=1, source_target_pairs={{0,4},{1,5},{2,6},{3,7},{4,0},{5,1},{6,2},{7,3},{8,12},{9,13},{10,... | collective-permute-start | bytes 1327112 | tf_op jit(solution)/shard_map/ppermute | solution.py:83
  444.2 27.2 %collective-permute-start.31 = (bf16[4,2,1,1,24,1280]{5,4,3,2,1,0:T(8,128)(2,1)S(1)}, bf16[4,2,1,1,24,1280]{5,4,3,2,1,0:T(8,128)(2,1)S(1)}, u32[]{:S(2)}, u32[]{:S(2)}) collective-permute-start(bf16[4,2,1,1,24,1280]{5,4,3,2,1,0:T(8,128)(2,1)S(1)} %constant_dynamic-slice_fusion.13), channel_id=1, source_target_pairs={{0,2},{1,3},{2,0},{3,1},{4,6},{5,7},{6,4},{7,5},{8,10},{9,11},{10,... | collective-permute-start | bytes 1474568 | tf_op jit(solution)/shard_map/ppermute | solution.py:83
  465.2 11.8 %collective-permute-start.29 = (bf16[4,1,1,1,24,1152]{5,4,3,2,1,0:T(8,128)(2,1)S(1)}, bf16[4,1,1,1,24,1152]{5,4,3,2,1,0:T(8,128)(2,1)S(1)}, u32[]{:S(2)}, u32[]{:S(2)}) collective-permute-start(bf16[4,1,1,1,24,1152]{5,4,3,2,1,0:T(8,128)(2,1)S(1)} %constant_dynamic-slice_fusion.15), channel_id=1, source_target_pairs={{0,2},{1,3},{2,0},{3,1},{4,6},{5,7},{6,4},{7,5},{8,10},{9,11},{10,... | collective-permute-start | bytes 663560 | tf_op jit(solution)/shard_map/ppermute | solution.py:83
  471.5 8.9 %collective-permute-start.32 = (bf16[4,1,1,1,24,1280]{5,4,3,2,1,0:T(8,128)(2,1)S(1)}, bf16[4,1,1,1,24,1280]{5,4,3,2,1,0:T(8,128)(2,1)S(1)}, u32[]{:S(2)}, u32[]{:S(2)}) collective-permute-start(bf16[4,1,1,1,24,1280]{5,4,3,2,1,0:T(8,128)(2,1)S(1)} %constant_dynamic-slice_fusion.12), channel_id=1, source_target_pairs={{0,4},{1,5},{2,6},{3,7},{4,0},{5,1},{6,2},{7,3},{8,12},{9,13},{10,... | collective-permute-start | bytes 737288 | tf_op jit(solution)/shard_map/ppermute | solution.py:83
  479.8 33.9 %collective-permute-start.37 = (bf16[4,1,2,1,24,3840]{5,4,3,2,1,0:T(8,128)(2,1)S(1)}, bf16[4,1,2,1,24,3840]{5,4,3,2,1,0:T(8,128)(2,1)}, u32[]{:S(2)}, u32[]{:S(2)}) collective-permute-start(bf16[4,1,2,1,24,3840]{5,4,3,2,1,0:T(8,128)(2,1)S(1)} %constant_dynamic-slice_fusion.10), channel_id=1, source_target_pairs={{0,4},{1,5},{2,6},{3,7},{4,0},{5,1},{6,2},{7,3},{8,12},{9,13},{10,... | collective-permute-start | bytes 4423688 | tf_op jit(solution)/shard_map/ppermute | solution.py:83
  480.6 6.2 %collective-permute-start.33 = (bf16[1,1,1,1,24,2432]{5,4,3,2,1,0:T(8,128)(2,1)S(1)}, bf16[1,1,1,1,24,2432]{5,4,3,2,1,0:T(8,128)(2,1)S(1)}, u32[]{:S(2)}, u32[]{:S(2)}) collective-permute-start(bf16[1,1,1,1,24,2432]{5,4,3,2,1,0:T(8,128)(2,1)S(1)} %get-tuple-element.93), channel_id=1, source_target_pairs={{0,8},{1,9},{2,10},{3,11},{4,12},{5,13},{6,14},{7,15},{8,0},{9,1},... | collective-permute-start | bytes 350216 | tf_op jit(solution)/shard_map/ppermute | solution.py:83
  480.7 6.8 %collective-permute-start.34 = (bf16[1,1,1,1,24,2432]{5,4,3,2,1,0:T(8,128)(2,1)S(1)}, bf16[1,1,1,1,24,2432]{5,4,3,2,1,0:T(8,128)(2,1)S(1)}, u32[]{:S(2)}, u32[]{:S(2)}) collective-permute-start(bf16[1,1,1,1,24,2432]{5,4,3,2,1,0:T(8,128)(2,1)S(1)} %get-tuple-element.94), channel_id=1, source_target_pairs={{0,16},{1,17},{2,18},{3,19},{4,20},{5,21},{6,22},{7,23},{8,24},{9,... | collective-permute-start | bytes 350216 | tf_op jit(solution)/shard_map/ppermute | solution.py:83
  480.9 12.7 %collective-permute-start.35 = (bf16[1,1,1,1,24,2432]{5,4,3,2,1,0:T(8,128)(2,1)S(1)}, bf16[1,1,1,1,24,2432]{5,4,3,2,1,0:T(8,128)(2,1)S(1)}, u32[]{:S(2)}, u32[]{:S(2)}) collective-permute-start(bf16[1,1,1,1,24,2432]{5,4,3,2,1,0:T(8,128)(2,1)S(1)} %get-tuple-element.95), channel_id=1, source_target_pairs={{0,24},{1,25},{2,26},{3,27},{4,28},{5,29},{6,30},{7,31},{8,16},{9,... | collective-permute-start | bytes 350216 | tf_op jit(solution)/shard_map/ppermute | solution.py:83
  516.8 17.2 %collective-permute-start.38 = (bf16[4,1,1,1,24,3840]{5,4,3,2,1,0:T(8,128)(2,1)}, bf16[4,1,1,1,24,3840]{5,4,3,2,1,0:T(8,128)(2,1)S(1)}, u32[]{:S(2)}, u32[]{:S(2)}) collective-permute-start(bf16[4,1,1,1,24,3840]{5,4,3,2,1,0:T(8,128)(2,1)} %constant_dynamic-slice_fusion.9), channel_id=1, source_target_pairs={{0,2},{1,3},{2,0},{3,1},{4,6},{5,7},{6,4},{7,5},{8,10},{9,11},{10,... | collective-permute-start | bytes 2211848 | tf_op jit(solution)/shard_map/ppermute | solution.py:83
  534.3 7.6 %collective-permute-start.39 = (bf16[1,1,1,1,24,3840]{5,4,3,2,1,0:T(8,128)(2,1)S(1)}, bf16[1,1,1,1,24,3840]{5,4,3,2,1,0:T(8,128)(2,1)S(1)}, u32[]{:S(2)}, u32[]{:S(2)}) collective-permute-start(bf16[1,1,1,1,24,3840]{5,4,3,2,1,0:T(8,128)(2,1)S(1)} %get-tuple-element.81), channel_id=1, source_target_pairs={{0,8},{1,9},{2,10},{3,11},{4,12},{5,13},{6,14},{7,15},{8,0},{9,1},... | collective-permute-start | bytes 552968 | tf_op jit(solution)/shard_map/ppermute | solution.py:83
  534.3 14.2 %collective-permute-start.41 = (bf16[1,1,1,1,24,3840]{5,4,3,2,1,0:T(8,128)(2,1)S(1)}, bf16[1,1,1,1,24,3840]{5,4,3,2,1,0:T(8,128)(2,1)S(1)}, u32[]{:S(2)}, u32[]{:S(2)}) collective-permute-start(bf16[1,1,1,1,24,3840]{5,4,3,2,1,0:T(8,128)(2,1)S(1)} %get-tuple-element.82), channel_id=1, source_target_pairs={{0,24},{1,25},{2,26},{3,27},{4,28},{5,29},{6,30},{7,31},{8,16},{9,... | collective-permute-start | bytes 552968 | tf_op jit(solution)/shard_map/ppermute | solution.py:83
  534.4 14.9 %collective-permute-start.40 = (bf16[1,1,1,1,24,3840]{5,4,3,2,1,0:T(8,128)(2,1)S(1)}, bf16[1,1,1,1,24,3840]{5,4,3,2,1,0:T(8,128)(2,1)S(1)}, u32[]{:S(2)}, u32[]{:S(2)}) collective-permute-start(bf16[1,1,1,1,24,3840]{5,4,3,2,1,0:T(8,128)(2,1)S(1)} %get-tuple-element.83), channel_id=1, source_target_pairs={{0,16},{1,17},{2,18},{3,19},{4,20},{5,21},{6,22},{7,23},{8,24},{9,... | collective-permute-start | bytes 552968 | tf_op jit(solution)/shard_map/ppermute | solution.py:83
  (74 other events, 1148.0 us)

commit v2 on v1

v2 whole, which is shorter than its diff:
```python
import jax
import jax.numpy as jnp
from jax import lax
from jax.experimental import pallas as pl
from jax.experimental.pallas import tpu as pltpu
from jax.sharding import PartitionSpec as P

D = 768
HEAD_DIM = 64
HEADS = D // HEAD_DIM
FF = 3072
SEQ_MOST = 1024
STEP = 10
VCOLS = 12


NORM_EPS = 1e-05
BETA_ONE = 0.9
BETA_TWO = 0.999
ADAM_EPS = 1e-08
DECAY_RATE = 0.01
NEG_LARGE = -1e30

LOW = jnp.bfloat16
FULL = jnp.float32


def norm_parts(values):
    centre = jnp.mean(values, axis=-1, keepdims=True)
    centred = values - centre
    spread = jnp.mean(centred * centred, axis=-1, keepdims=True)
    inverse = lax.rsqrt(spread + NORM_EPS)
    return centred * inverse, inverse


def norm_back(grad, unit, inverse, gain_vec):
    scaled = grad * gain_vec
    along = jnp.mean(scaled * unit, axis=-1, keepdims=True)
    return inverse * (scaled - jnp.mean(scaled, axis=-1, keepdims=True) - unit * along)


def smooth_act(values):
    return jax.nn.gelu(values, approximate=True)


def adamw(weight, moment, second, gradient, step_rate, decay_rate):
    moment = BETA_ONE * moment + (1.0 - BETA_ONE) * gradient
    second = BETA_TWO * second + (1.0 - BETA_TWO) * gradient * gradient
    first_hat = moment / (1.0 - BETA_ONE**STEP)
    second_hat = second / (1.0 - BETA_TWO**STEP)
    weight = weight - step_rate * (
        first_hat / (jnp.sqrt(second_hat) + ADAM_EPS) + decay_rate * weight
    )
    return (moment, second, weight)


def matrix_rates():
    return (
        2.5 * D ** (-0.5),
        2.5 * max(1, D * 16 // SEQ_MOST) ** (-0.5),
        2.5 * D ** (-0.5),
        2.5 * FF ** (-0.5),
    )


def vector_rates(entries):
    column = entries % 8
    is_gain = (entries < 8 * D) & ((column == 0) | (column == 5))
    return jnp.where(is_gain, 0.3, 0.05).astype(jnp.float32)


def shifted(x, by):
    length = lax.axis_size("dev")
    return lax.ppermute(x, "dev", [(i, i + by) for i in range(length) if 0 <= i + by < length])


def flipped(x, mask):
    return lax.ppermute(x, "dev", [(i, i ^ mask) for i in range(lax.axis_size("dev"))])


def tied(*arrays):
    return lax.optimization_barrier(arrays)


class Index:
    def __init__(self):
        self.count = lax.axis_size("dev")
        self.me = lax.axis_index("dev")
        self.top = self.count.bit_length() - 3
        self.core = self.me & 1
        self.odd = self.core == 1
        middle = tuple(range(1, self.top))
        self.orders = (middle, tuple(reversed(middle)))

    def relative(self, order):
        seen = [r << self.top for r in range(4)]
        for b in reversed(order):
            seen = seen + [s | 1 << b for s in seen]
        return [s >> 1 for s in seen]


def by_core(ix, own, other):
    return jnp.where(ix.odd, other, own), jnp.where(ix.odd, own, other)


def cut_sides(x):
    cut = x.shape[-1] // 256 * 128
    return (x[..., :cut], x[..., cut:])


def gather_top(ix, piece):
    return jnp.stack([piece] + [flipped(piece, r << ix.top) for r in (1, 2, 3)])


def gather_mid(ix, sides):
    done = []
    for x, order in zip(sides, ix.orders):
        for b in reversed(order[1:]):
            x = jnp.concatenate([x, flipped(x, 1 << b)], axis=0)
        done.append(x)
    return done


def gather_last(ix, sides):
    return [(x, flipped(x, 1 << order[0])) for x, order in zip(sides, ix.orders)]


def place_kernel(rows, moves, chip_ref, *refs):
    ins, outs, sem = refs[: moves[0]], refs[moves[0] : -1], refs[-1]
    chip = chip_ref[0]
    copies = []
    for source, at, target, relative, column, width in moves[1]:
        start = pl.multiple_of((chip ^ relative) * rows, rows)
        spot = (pl.ds(start, rows), pl.ds(column, width))
        if at[0] == 0:
            copy = (ins[source].at[at[1]], outs[target].at[spot])
        else:
            copy = (ins[source].at[spot], outs[target].at[at[1]])
        copies.append(pltpu.make_async_copy(*copy, sem.at[len(copies)]))
        copies[-1].start()
    for copy in copies:
        copy.wait()


def place(ix, rows, ins, moves, out_shape):
    return pl.pallas_call(
        lambda *refs: place_kernel(rows, (len(ins), moves), *refs),
        in_specs=[pl.BlockSpec(memory_space=pltpu.SMEM)]
        + [pl.BlockSpec(memory_space=pl.ANY)] * len(ins),
        out_specs=[pl.BlockSpec(memory_space=pl.ANY)] * len(out_shape),
        out_shape=[jax.ShapeDtypeStruct(shape, LOW) for shape in out_shape],
        scratch_shapes=[pltpu.SemaphoreType.DMA((len(moves),))],
        cost_estimate=pl.CostEstimate(
            flops=0, bytes_accessed=4 * sum(rows * m[5] for m in moves), transcendentals=0
        ),
    )((ix.me >> 1).astype(jnp.int32).reshape(1), *ins)


def assemble(ix, sides):
    chips = ix.count // 2
    rows = sides[0][0].shape[1]
    widths = [side[0].shape[2] for side in sides]
    if rows % 16:
        whole = []
        for side, order in zip(sides, ix.orders):
            place_of = [0] * chips
            for spot, relative in enumerate(ix.relative(order)):
                place_of[relative] = spot
            pick = jnp.array(place_of, jnp.int32)[(ix.me >> 1) ^ jnp.arange(chips)]
            full = jnp.take(jnp.concatenate(side, axis=0), pick, axis=0)
            whole.append(full.reshape(chips * rows, -1))
        return jnp.concatenate(whole, axis=1)
    moves = []
    for s, order in enumerate(ix.orders):
        for spot, relative in enumerate(ix.relative(order)):
            half, at = divmod(spot, chips // 2)
            moves.append((2 * s + half, (0, at), 0, relative, s * widths[0], widths[s]))
    ins = [array for side in sides for array in side]
    return place(ix, rows, ins, moves, [(chips * rows, sum(widths))])[0]


def take_apart(ix, whole):
    chips = ix.count // 2
    rows = whole.shape[0] // chips
    if rows % 16:
        sides = []
        for side, order in zip(cut_sides(whole), ix.orders):
            pick = (ix.me >> 1) ^ jnp.array(ix.relative(order), jnp.int32)
            full = jnp.take(side.reshape(chips, rows, -1), pick, axis=0)
            sides.append((full[: chips // 2], full[chips // 2 :]))
        return sides
    widths = [side.shape[1] for side in cut_sides(whole)]
    moves, shapes = [], []
    for s, order in enumerate(ix.orders):
        shapes += [(chips // 2, rows, widths[s])] * 2
        for spot, relative in enumerate(ix.relative(order)):
            half, at = divmod(spot, chips // 2)
            moves.append((0, (1, at), 2 * s + half, relative, s * widths[0], widths[s]))
    outs = place(ix, rows, [whole], moves, shapes)
    return [(outs[0], outs[1]), (outs[2], outs[3])]


def settle(keep, other, parts):
    size = keep.shape[0] // parts
    return [
        (
            keep[i * size : (i + 1) * size].astype(FULL)
            + other[i * size : (i + 1) * size].astype(FULL)
        ).astype(LOW)
        for i in range(parts)
    ]


def scatter_mid(ix, sides, first, last):
    done = []
    for (keep, send), order in zip(sides, ix.orders):
        for i in range(first, min(last, len(order))):
            parts = 2 if i < len(order) - 1 else 4
            settled = settle(keep, flipped(send, 1 << order[i]), parts)
            keep, send = settled[0], settled[1] if parts == 2 else settled[1:]
        done.append((keep, send))
    return done


def scatter_top(ix, sides):
    total = jnp.concatenate([keep[0] for keep, _ in sides], axis=-1).astype(FULL)
    for r in (1, 2, 3):
        part = jnp.concatenate([send[r - 1][0] for _, send in sides], axis=-1)
        total = total + flipped(part, r << ix.top).astype(FULL)
    return total


def own_rows(ix, summed):
    rows = summed.shape[0] // 2
    keep = lax.dynamic_slice_in_dim(summed, ix.core * rows, rows, 0)
    other = lax.dynamic_slice_in_dim(summed, (1 - ix.core) * rows, rows, 0)
    return keep, flipped(other, 1)


PAIR = 2 * HEAD_DIM
PAIRS = HEADS // 2
SIDE = PAIRS // 2
SCALE = HEAD_DIM ** (-0.5)
VMEM_BYTES = 48 * 1024 * 1024


def by_head(pair):
    low_half = lax.broadcasted_iota(jnp.int32, pair.shape, 1) < HEAD_DIM
    zero = jnp.zeros_like(pair)
    return (
        low_half,
        jnp.where(low_half, pair, zero).astype(LOW),
        jnp.where(low_half, zero, pair).astype(LOW),
    )


def dot_over(operand_a, operand_b, dim_a, dim_b):
    return lax.dot_general(
        operand_a, operand_b, (((dim_a,), (dim_b,)), ((), ())), preferred_element_type=FULL
    )


def attend_kernel(first_ref, q_ref, kv_ref, out_ref, weights_ref):
    rows, near = weights_ref.shape[-2:]
    key = lax.broadcasted_iota(jnp.int32, (rows, near), 1)
    last = lax.broadcasted_iota(jnp.int32, (rows, near), 0) + (near - rows)
    for block in range(2):
        own, seen = pl.ds(block * rows, rows), pl.ds(block * rows, near)
        low_half, *q_heads = by_head(q_ref[own, :].astype(FULL) * SCALE)
        k, v = kv_ref[seen, :PAIR], kv_ref[seen, PAIR:]
        allowed = (key >= first_ref[own, :] - block * rows) & (key <= last)
        blended = []
        for head in range(2):
            scores = jnp.where(allowed, dot_over(q_heads[head], k, 1, 1), NEG_LARGE)
            weights = jnp.exp(scores - jnp.max(scores, axis=-1, keepdims=True))
            weights = weights * (1.0 / jnp.sum(weights, axis=-1, keepdims=True))
            weights = weights.astype(LOW)
            weights_ref[0, 2 * block + head] = weights
            blended.append(dot_over(weights, v, 1, 0))
        out_ref[own, :] = jnp.where(low_half, blended[0], blended[1]).astype(LOW)


def attend(first_key, query, kv, rows, first, pairs):
    near = kv.shape[0] - rows
    return pl.pallas_call(
        attend_kernel,
        grid=(pairs,),
        in_specs=[
            pl.BlockSpec((2 * rows, 1), lambda i: (0, 0)),
            pl.BlockSpec((2 * rows, PAIR), lambda i: (0, i + first)),
            pl.BlockSpec((near + rows, 2 * PAIR), lambda i: (0, i + first)),
        ],
        out_specs=[
            pl.BlockSpec((2 * rows, PAIR), lambda i: (0, i)),
            pl.BlockSpec((1, 4, rows, near), lambda i: (i, 0, 0, 0)),
        ],
        out_shape=[
            jax.ShapeDtypeStruct((2 * rows, pairs * PAIR), LOW),
            jax.ShapeDtypeStruct((pairs, 4, rows, near), LOW),
        ],
        compiler_params=pltpu.CompilerParams(vmem_limit_bytes=VMEM_BYTES),
        cost_estimate=pl.CostEstimate(
            flops=32 * pairs * rows * near * PAIR,
            bytes_accessed=16 * pairs * rows * near,
            transcendentals=4 * pairs * rows * near,
        ),
    )(first_key, query, kv)


def attend_back_kernel(weights_ref, grad_ref, q_ref, kv_ref, dq_ref, dkv_ref):
    rows, near = weights_ref.shape[-2:]
    turned = []
    for block in range(2):
        own, seen = pl.ds(block * rows, rows), pl.ds(block * rows, near)
        low_half, *grad_heads = by_head(grad_ref[own, :].astype(FULL))
        _, *q_heads = by_head(q_ref[own, :].astype(FULL))
        k, v = kv_ref[seen, :PAIR], kv_ref[seen, PAIR:]
        dq = []
        dk_turned = dv_turned = 0.0
        for head in range(2):
            weights_low = weights_ref[0, 2 * block + head]
            weights = weights_low.astype(FULL)
            grad_weights = dot_over(grad_heads[head], v, 1, 1)
            inner_sum = jnp.sum(weights * grad_weights, axis=-1, keepdims=True)
            grad_scores = (weights * (grad_weights - inner_sum)).astype(LOW)
            dq.append(dot_over(grad_scores, k, 1, 0))
            dk_turned += dot_over(q_heads[head], grad_scores, 0, 0)
            dv_turned += dot_over(grad_heads[head], weights_low, 0, 0)
        dq_ref[own, :] = (jnp.where(low_half, dq[0], dq[1]) * SCALE).astype(LOW)
        turned.append((dk_turned * SCALE, dv_turned))
    for which in range(2):
        early, late = turned[0][which], turned[1][which]
        whole = jnp.concatenate(
            [early[:, :rows], early[:, rows:] + late[:, : near - rows], late[:, near - rows :]],
            axis=1,
        )
        dkv_ref[:, which * PAIR : (which + 1) * PAIR] = whole.T.astype(LOW)


def attend_back(weights, grad, query, kv, rows, first, pairs):
    near = kv.shape[0] - rows
    return pl.pallas_call(
        attend_back_kernel,
        grid=(pairs,),
        in_specs=[
            pl.BlockSpec((1, 4, rows, near), lambda i: (i, 0, 0, 0)),
            pl.BlockSpec((2 * rows, PAIR), lambda i: (0, i + first)),
            pl.BlockSpec((2 * rows, PAIR), lambda i: (0, i + first)),
            pl.BlockSpec((near + rows, 2 * PAIR), lambda i: (0, i + first)),
        ],
        out_specs=[
            pl.BlockSpec((2 * rows, PAIR), lambda i: (0, i)),
            pl.BlockSpec((near + rows, 2 * PAIR), lambda i: (0, i)),
        ],
        out_shape=[
            jax.ShapeDtypeStruct((2 * rows, pairs * PAIR), LOW),
            jax.ShapeDtypeStruct((near + rows, 2 * pairs * PAIR), LOW),
        ],
        compiler_params=pltpu.CompilerParams(vmem_limit_bytes=VMEM_BYTES),
        cost_estimate=pl.CostEstimate(
            flops=64 * pairs * rows * near * PAIR,
            bytes_accessed=16 * pairs * rows * near,
            transcendentals=0,
        ),
    )(weights, grad, query, kv)


def paired_columns(x):
    rows = x.shape[0]
    query = x[:, :D].reshape(rows, 2, SIDE * PAIR)
    kv = x[:, D:].reshape(rows, 2, 2, SIDE, PAIR).transpose(0, 2, 3, 1, 4)
    kv = kv.reshape(rows, 2, 2 * SIDE * PAIR)
    return [jnp.concatenate([query[:, s], kv[:, s]], axis=1) for s in range(2)]


def plain_columns(sides):
    rows, wide = sides[0].shape[0], SIDE * PAIR
    query = [side[:, :wide] for side in sides]
    kv = [side[:, wide:].reshape(rows, SIDE, 2, PAIR).transpose(0, 2, 1, 3) for side in sides]
    key_value = [kv[s][:, which].reshape(rows, wide) for which in range(2) for s in range(2)]
    return jnp.concatenate(query + key_value, axis=1)


def hidden_columns(x, share):
    parts = x.reshape(x.shape[0], FF // (2 * share), 2, share)
    return [parts[:, :, s].reshape(x.shape[0], FF // 2) for s in range(2)]


def plain_hidden(sides, share):
    rows = sides[0].shape[0]
    parts = [side.reshape(rows, FF // (2 * share), 1, share) for side in sides]
    return jnp.concatenate(parts, axis=2).reshape(rows, FF)


def dot(operand_a, operand_b):
    return jnp.dot(operand_a, operand_b, preferred_element_type=FULL)


def outer_sum(operand_a, operand_b):
    return jnp.einsum("ti,tj->ij", operand_a, operand_b, preferred_element_type=FULL).astype(LOW)


def dot_turned(operand_a, operand_b):
    return jnp.einsum("ti,ji->tj", operand_a, operand_b, preferred_element_type=FULL)


def body(
    tokens,
    cotangent,
    starts,
    w_qkv,
    m_qkv,
    v_qkv,
    w_out,
    m_out,
    v_out,
    w_up,
    m_up,
    v_up,
    w_down,
    m_down,
    v_down,
    vectors,
    m_vec,
    v_vec,
):
    ix = Index()
    rows = D // ix.count
    share = FF // ix.count
    tok_rows = tokens.shape[0]
    reach_count = (SEQ_MOST + tok_rows - 2) // tok_rows
    assert reach_count == 4
    chip_rows = 2 * tok_rows
    near_rows = (reach_count + 2) * tok_rows
    wide = SIDE * PAIR
    columns = 3 * wide
    out_wide, up_wide = D // 2, FF // 2

    vec_piece = jnp.pad(vectors.astype(LOW).reshape(rows, VCOLS), ((0, 0), (0, 128 - VCOLS)))
    qkv_sides = paired_columns(w_qkv.astype(LOW).reshape(rows, 3 * D))
    up_sides = hidden_columns(w_up.astype(LOW).reshape(rows, FF), share)
    out_low = w_out.astype(LOW).reshape(rows, D)
    pieces = [
        jnp.concatenate(
            [qkv_sides[s], vec_piece, out_low[:, s * out_wide : (s + 1) * out_wide], up_sides[s]],
            axis=1,
        )
        for s in range(2)
    ]
    mine, others = by_core(ix, *pieces)
    both = jnp.concatenate(by_core(ix, mine, flipped(others, 1)), axis=0)
    first, second = both[:, : columns + 128], both[:, columns + 128 :]
    first = gather_top(ix, first)

    mine = jnp.stack([shifted(tokens, 4), shifted(tokens, 2), tokens])
    near_tokens = jnp.stack(by_core(ix, mine, flipped(mine, 1)), axis=1).reshape(near_rows, D)
    chip_starts = jnp.concatenate(by_core(ix, starts, flipped(starts, 1)))
    chip_cotangent = jnp.concatenate(by_core(ix, cotangent, flipped(cotangent, 1)), axis=0)

    first, second, near_tokens, chip_starts = tied(first, second, near_tokens, chip_starts)
    second = gather_top(ix, second)
    first = gather_last(ix, gather_mid(ix, cut_sides(first)))
    third = w_down.astype(LOW).reshape(4 * rows, D)
    first, second, third, chip_cotangent = tied(first, second, third, chip_cotangent)
    third = gather_top(ix, third)
    second = gather_mid(ix, cut_sides(second))
    first = assemble(ix, first)
    qkv_w = first[:, :columns]
    vec_all = first[:, columns : columns + VCOLS].reshape(-1).astype(FULL)
    vec_table, up_bias = vec_all[: 8 * D].reshape(D, 8).T, vec_all[8 * D :]
    gain_one, shift_one, bias_q, bias_v, bias_o, gain_two, shift_two, bias_down = (
        vec_table[i] for i in range(8)
    )
    up_bias = lax.dynamic_index_in_dim(
        up_bias.reshape(ix.count // 2, 2, share), ix.core, 1, keepdims=False
    ).reshape(up_wide)
    bias_q = lax.dynamic_slice_in_dim(bias_q, ix.core * wide, wide)
    bias_v = lax.dynamic_slice_in_dim(bias_v, ix.core * wide, wide)

    near_unit, near_inverse = norm_parts(near_tokens.astype(FULL))
    near_normed = (near_unit * gain_one + shift_one).astype(LOW)
    normed = near_normed[near_rows - chip_rows :]
    kv_bias = jnp.stack(
        [jnp.zeros((SIDE, PAIR), FULL), bias_v.reshape(SIDE, PAIR)], axis=1
    ).reshape(2 * wide)
    first_key = (chip_starts - ((ix.me >> 1) * chip_rows - reach_count * tok_rows))[:, None]
    query = (dot(normed, qkv_w[:, :wide]) + bias_q).astype(LOW)
    kv = (dot(near_normed, qkv_w[:, wide:]) + kv_bias).astype(LOW)
    query, kv, second = tied(query, kv, second)
    second = gather_last(ix, second)
    splits = ((0, SIDE - 1), (SIDE - 1, 1))
    mixed, weights = [None, None], [None, None]
    mixed[0], weights[0] = attend(first_key, query, kv, tok_rows, *splits[0])
    mixed[0], query, third = tied(mixed[0], query, third)
    third = gather_mid(ix, cut_sides(third))
    mixed[1], weights[1] = attend(first_key, query, kv, tok_rows, *splits[1])
    mixed = jnp.concatenate(mixed, axis=1)
    mixed, second, third = tied(mixed, second, third)
    third = gather_last(ix, third)
    attended = jnp.concatenate(by_core(ix, mixed, flipped(mixed, 1)), axis=1)
    second = assemble(ix, second)
    out_half, up_w = second[:, :out_wide], second[:, out_wide:]
    out_w = jnp.concatenate(by_core(ix, out_half, flipped(out_half, 1)), axis=1)

    inputs = near_tokens[near_rows - chip_rows :].astype(FULL)
    middle = inputs + (dot(attended, out_w) + bias_o)
    unit_two, inverse_two = norm_parts(middle)
    normed_two = (unit_two * gain_two + shift_two).astype(LOW)
    hidden_pre = dot(normed_two, up_w) + up_bias
    hidden_low = smooth_act(hidden_pre).astype(LOW)
    grad_downw = outer_sum(hidden_low, chip_cotangent)
    hidden_low, hidden_pre, grad_downw = tied(hidden_low, hidden_pre, grad_downw)
    sum_down = scatter_mid(ix, take_apart(ix, grad_downw), 0, 1)
    down_w = assemble(ix, third)
    result = dot(hidden_low, down_w).reshape(2, tok_rows, D)
    own_result, other_result = by_core(ix, result[0], result[1])
    own_result = own_result + flipped(other_result.astype(LOW), 1).astype(FULL)
    own_middle = lax.dynamic_slice_in_dim(middle, ix.core * tok_rows, tok_rows, 0)
    out_tokens = (own_middle + (own_result + bias_down)).astype(LOW)

    grad_hidden = dot_turned(chip_cotangent, down_w)
    act_value, act_back = jax.vjp(smooth_act, hidden_pre)
    grad_pre = act_back(grad_hidden)[0].astype(LOW)
    partial_two = dot_turned(grad_pre, up_w)
    grad_gain_two = jnp.sum(partial_two * unit_two, axis=0)
    grad_shift_two = jnp.sum(partial_two, axis=0)
    grad_normed_two = partial_two + flipped(partial_two.astype(LOW), 1).astype(FULL)
    grad_upw = outer_sum(normed_two, grad_pre)
    grad_middle = chip_cotangent.astype(FULL) + norm_back(
        grad_normed_two, unit_two, inverse_two, gain_two
    )
    grad_branch = grad_middle.astype(LOW)
    own_part = lax.dynamic_slice_in_dim(grad_branch, ix.core * out_wide, out_wide, 1)
    grad_second = jnp.concatenate([outer_sum(attended, own_part), grad_upw], axis=1)
    own_out = lax.dynamic_slice_in_dim(out_w, ix.core * wide, wide, 0)
    grad_mixed = dot_turned(grad_branch, own_out).astype(LOW)
    grad_mixed, grad_second, sum_down = tied(grad_mixed, grad_second, sum_down)
    sum_second = scatter_mid(ix, take_apart(ix, grad_second), 0, 1)
    sum_down = scatter_mid(ix, sum_down, 1, 9)
    dq, dkv = [None, None], [None, None]
    dq[0], dkv[0] = attend_back(weights[0], grad_mixed, query, kv, tok_rows, *splits[0])
    dq[0], dkv[0], grad_mixed, sum_down = tied(dq[0], dkv[0], grad_mixed, sum_down)
    sum_down = scatter_top(ix, sum_down)
    dq[1], dkv[1] = attend_back(weights[1], grad_mixed, query, kv, tok_rows, *splits[1])
    dq, dkv = jnp.concatenate(dq, axis=1), jnp.concatenate(dkv, axis=1)
    dq, dkv, sum_second = tied(dq, dkv, sum_second)
    sum_second = scatter_mid(ix, sum_second, 1, 9)

    grad_near = dot_turned(dkv, qkv_w[:, wide:]) + jnp.pad(
        dot_turned(dq, qkv_w[:, :wide]), ((near_rows - chip_rows, 0), (0, 0))
    )
    grad_gain_one = jnp.sum(grad_near * near_unit, axis=0)
    grad_shift_one = jnp.sum(grad_near, axis=0)
    own_half = (jnp.arange(2) == ix.core).astype(FULL)[:, None]
    grad_bias_v = jnp.sum(dkv.astype(FULL), axis=0).reshape(SIDE, 2, PAIR)[:, 1].reshape(1, wide)
    vec_rows = jnp.stack(
        [
            grad_gain_one,
            grad_shift_one,
            (jnp.sum(dq.astype(FULL), axis=0)[None] * own_half).reshape(D),
            (grad_bias_v * own_half).reshape(D),
            0.5 * jnp.sum(grad_branch.astype(FULL), axis=0),
            grad_gain_two,
            grad_shift_two,
            jnp.sum(cotangent.astype(FULL), axis=0),
        ],
        axis=0,
    )
    grad_bias_up = jnp.sum(grad_pre.astype(FULL), axis=0).reshape(ix.count // 2, 1, share)
    grad_vec = jnp.concatenate([vec_rows.T.reshape(-1), (grad_bias_up * own_half).reshape(-1)])
    grad_vec = lax.optimization_barrier(grad_vec).astype(LOW).reshape(D, VCOLS)
    grad_vec = jnp.pad(grad_vec, ((0, 0), (0, 128 - VCOLS)))
    grad_first = jnp.concatenate(
        [outer_sum(normed, dq), outer_sum(near_normed, dkv), grad_vec], axis=1
    )
    sum_first = scatter_mid(ix, take_apart(ix, grad_first), 0, 1)
    sum_second = scatter_top(ix, sum_second)
    sum_first = scatter_mid(ix, sum_first, 1, 9)

    blocks = grad_near.reshape(reach_count // 2 + 1, 2, tok_rows, D)
    own_blocks, other_blocks = by_core(ix, blocks[:, 0], blocks[:, 1])
    own_blocks = own_blocks + flipped(other_blocks.astype(LOW), 1).astype(FULL)
    four_back, two_back = own_blocks[0].astype(LOW), own_blocks[1].astype(LOW)
    own = (
        own_blocks[2]
        + shifted(two_back, -2).astype(FULL)
        + shifted(four_back, -4).astype(FULL)
    )
    unit_one, inverse_one = norm_parts(tokens.astype(FULL))
    own_grad_middle = lax.dynamic_slice_in_dim(grad_middle, ix.core * tok_rows, tok_rows, 0)
    input_grad = own_grad_middle + norm_back(own, unit_one, inverse_one, gain_one)

    sum_first = scatter_top(ix, sum_first)
    keep_second, other_second = own_rows(ix, sum_second)
    keep_first, other_first = own_rows(ix, sum_first)
    g_vec = (keep_first[:, columns:] + other_first[:, columns:])[:, :VCOLS].reshape(-1)
    g_qkv = plain_columns(by_core(ix, keep_first[:, :columns], other_first[:, :columns]))
    g_out = jnp.concatenate(
        by_core(ix, keep_second[:, :out_wide], other_second[:, :out_wide]), axis=1
    )
    g_up = plain_hidden(by_core(ix, keep_second[:, out_wide:], other_second[:, out_wide:]), share)

    rate_qkv, rate_out, rate_up, rate_down = matrix_rates()
    entries = ix.me * vectors.shape[0] + jnp.arange(vectors.shape[0], dtype=jnp.int32)
    qkv_new = adamw(w_qkv, m_qkv, v_qkv, g_qkv.reshape(-1), rate_qkv, DECAY_RATE)
    out_new = adamw(w_out, m_out, v_out, g_out.reshape(-1), rate_out, DECAY_RATE)
    up_new = adamw(w_up, m_up, v_up, g_up.reshape(-1), rate_up, DECAY_RATE)
    down_new = adamw(w_down, m_down, v_down, sum_down.reshape(-1), rate_down, DECAY_RATE)
    vec_new = adamw(vectors, m_vec, v_vec, g_vec, vector_rates(entries), 0.0)
    return (out_tokens, input_grad) + qkv_new + out_new + up_new + down_new + vec_new


def solution(mesh):
    in_specs = (P("dev", None), P("dev", None)) + (P("dev"),) * 16
    out_specs = (P("dev", None), P("dev", None)) + (P("dev"),) * 15
    return jax.shard_map(body, mesh=mesh, in_specs=in_specs, out_specs=out_specs, check_vma=False)
```

time: 563 us -> 811 us (1.44)
  Pallas kernels: 0 us -> 475 us
  waiting for transfers between devices: 239 us -> 114 us
  matrix products: 150 us -> 41.5 us
  other arithmetic: 51.2 us -> 76.5 us
  local copies, waits for them, and re-layouts: 41.6 us -> 28 us
    pallas_call x0 -> x10, Pallas kernels: none -> 475 us  [the longest x6 449 us: place(): pl.pallas_call(lambda *refs: place_kernel(rows, (len(ins), moves), *refs)...]
    ppermute x44 -> x53, waiting for transfers between devices: 222 us -> 85.3 us  [flipped(): lax.ppermute(x, 'dev', [(i, i ^ mask) for i in range(lax.axis_size('dev'))])]
    dot_general x15 -> x10, matrix products: 122 us -> 30.3 us  [the longest x5 20 us: dot_turned(): jnp.einsum('ti,ji->tj', operand_a, operand_b, preferred_element_type=FULL)]
    ppermute x4, waiting for transfers between devices: 16.8 us -> 29.2 us  [shifted(): lax.ppermute(x, 'dev', [(i, i + by) for i in range(length) if 0 <= i + by...]
    sub x1 -> x0, matrix products: 10.5 us -> none  [body(): weights = jnp.exp(scores - peak)]
    convert_element_type x17 -> x16, other arithmetic: 15.8 us -> 17.8 us  [the longest x8 9 us: settle(): return [(keep[i * size:(i + 1) * size].astype(FULL) + other[i * size:(i +...]
    ppermute x44 -> x53, starting transfers between devices: 53.4 us -> 52.1 us  [flipped(): lax.ppermute(x, 'dev', [(i, i ^ mask) for i in range(lax.axis_size('dev'))])]
  transfers between devices with their start and end apart: 48 -> 57, of which waited for: 28 -> 23; matrix products, arithmetic and copies ran while one was open for 17% -> 13% of each run, Pallas kernels for 0% -> 47%
where the time goes in v2:
time: 811 us; the launch traced here: 803 us
  Pallas kernels  475 us (59%)
  waiting for transfers between devices  114 us (14%)
  other arithmetic  76.5 us (9%)
  starting transfers between devices  64.3 us (8%)
  matrix products  41.5 us (5%)
  local copies, waits for them, and re-layouts  28 us (3%)
    pallas_call x6, Pallas kernels, place(): pl.pallas_call(lambda *refs: place_kernel(rows, (len(ins), moves), *refs)...  449 us
    ppermute x53, waiting for transfers between devices, flipped(): lax.ppermute(x, 'dev', [(i, i ^ mask) for i in range(lax.axis_size('dev'))])  85.3 us
    ppermute x53, starting transfers between devices, flipped(): lax.ppermute(x, 'dev', [(i, i ^ mask) for i in range(lax.axis_size('dev'))])  52.1 us
    ppermute x4, waiting for transfers between devices, shifted(): lax.ppermute(x, 'dev', [(i, i + by) for i in range(length) if 0 <= i + by...  29.2 us
    dot_general x5, matrix products, dot_turned(): jnp.einsum('ti,ji->tj', operand_a, operand_b, preferred_element_type=FULL)  20 us
  transfers between devices with their start and end apart: 57, of which 23 were waited for; matrix products, arithmetic and copies ran while one was open for 13% of the time, Pallas kernels for 47%

profile of v2, /device:TPU:12, one launch (start us, length us, event | category | flops | bytes accessed | tf_op | source)
XLA Modules:
  0.0 803.0 jit_solution(10818199905718620766)
XLA Ops:
  0.7 3.5 collective-permute-start.5
  4.2 3.4 collective-permute-start.4
  15.4 7.7 collective-permute-done.4
  23.9 2.6 collective-permute-start.2
  29.4 6.1 collective-permute-done.2
  35.5 2.8 collective-permute-done.3
  41.1 3.0 collective-permute-start.13
  61.4 3.1 collective-permute-done.11.refs_4_
  73.5 61.0 %shard_map.305 = bf16[768,1280]{1,0:T(8,128)(2,1)} custom-call(s32[1]{0:T(128)} %bitcast.16.refs_0_, bf16[8,48,640]{2,1,0:T(8,128)(2,1)} %pad_maximum_fusion.17.refs_1_, bf16[8,48,640]{2,1,0:T(8,128)(2,1)} %collective-permute-done.9.refs_2_, bf16[8,48,640]{2,1,0:T(8,128)(2,1)} %pad_maximum_fusion.18.refs_3_, bf16[8,48,640]{2,1,0:T(8,128)(2,1)} %collective-permute-done.11.refs_4_), custom_call_target="tpu_custom_call" | custom-call | bytes 3932160 | tf_op jit(solution)/shard_map/pallas_call | solution.py:146
  149.5 9.1 %shard_map.306 = (bf16[512,256]{1,0:T(8,128)(2,1)S(1)}, bf16[2,4,256,1280]{3,2,1,0:T(8,128)(2,1)}) custom-call(s32[512,1]{1,0:T(8,128)S(1)} %copy.60.first_ref, bf16[512,384]{1,0:T(8,128)(2,1)S(1)} %fusion.28.q_ref, bf16[1536,768]{1,0:T(8,128)(2,1)S(1)} %add_convert_fusion.kv_ref), custom_call_target="tpu_custom_call" | custom-call | flops 2684354560 | bytes 10485760 | tf_op jit(solution)/shard_map/pallas_call | solution.py:285
  163.5 3.6 shard_map.307
  171.4 8.6 %collective-permute-done.23 = bf16[4,96,384]{2,1,0:T(8,128)(2,1)S(1)} collective-permute-done((bf16[4,96,384]{2,1,0:T(8,128)(2,1)S(1)}, bf16[4,96,384]{2,1,0:T(8,128)(2,1)S(1)}, u32[]{:S(2)}, u32[]{:S(2)}) %collective-permute-start.23) | collective-permute-done | bytes 294944 | tf_op jit(solution)/shard_map/ppermute | solution.py:78
  182.8 90.7 %shard_map.308 = bf16[768,1920]{1,0:T(8,128)(2,1)} custom-call(s32[1]{0:T(128)} %bitcast.16.refs_0_, bf16[8,48,896]{2,1,0:T(8,128)(2,1)} %copy-done.17, bf16[8,48,896]{2,1,0:T(8,128)(2,1)} %copy-done.32, bf16[8,48,1024]{2,1,0:T(8,128)(2,1)} %copy-done.16, bf16[8,48,1024]{2,1,0:T(8,128)(2,1)} %copy-done.30), custom_call_target="tpu_custom_call" | custom-call | bytes 5898240 | tf_op jit(solution)/shard_map/pallas_call | solution.py:146
  288.8 3.9 fusion.23
  292.7 2.9 convolution_convert_fusion.1.refs_1_
  295.6 72.9 %shard_map.310 = (bf16[8,96,384]{2,1,0:T(8,128)(2,1)}, bf16[8,96,384]{2,1,0:T(8,128)(2,1)}, bf16[8,96,384]{2,1,0:T(8,128)(2,1)}, bf16[8,96,384]{2,1,0:T(8,128)(2,1)}) custom-call(s32[1]{0:T(128)} %bitcast.16.refs_0_, bf16[1536,768]{1,0:T(8,128)(2,1)} %convolution_convert_fusion.1.refs_1_), custom_call_target="tpu_custom_call" | custom-call | bytes 4718592 | tf_op jit(solution)/shard_map/pallas_call | solution.py:146
  368.8 72.9 %shard_map.309 = bf16[1536,768]{1,0:T(8,128)(2,1)} custom-call(s32[1]{0:T(128)} %bitcast.16.refs_0_, bf16[8,96,384]{2,1,0:T(8,128)(2,1)} %pad_maximum_fusion.12.refs_1_, bf16[8,96,384]{2,1,0:T(8,128)(2,1)} %collective-permute-done.27.refs_2_, bf16[8,96,384]{2,1,0:T(8,128)(2,1)} %pad_maximum_fusion.13.refs_3_, bf16[8,96,384]{2,1,0:T(8,128)(2,1)} %collective-permute-done.28.refs_4_), custom_call_target="tpu_custom_call" | custom-call | bytes 4718592 | tf_op jit(solution)/shard_map/pallas_call | solution.py:146
  441.7 6.8 convert_reduce_fusion.2
  448.5 2.8 fusion.100
  454.0 3.1 convolution_convert_fusion
  461.6 2.7 add_convert_fusion.4
  466.6 6.6 collective-permute-done.31
  475.2 2.7 multiply_reduce_fusion
  477.9 3.1 convert_reduce_fusion.3
  485.0 90.7 %shard_map.313 = (bf16[8,48,896]{2,1,0:T(8,128)(2,1)}, bf16[8,48,896]{2,1,0:T(8,128)(2,1)}, bf16[8,48,1024]{2,1,0:T(8,128)(2,1)}, bf16[8,48,1024]{2,1,0:T(8,128)(2,1)}) custom-call(s32[1]{0:T(128)} %bitcast.16.refs_0_, bf16[768,1920]{1,0:T(8,128)(2,1)} %pad_maximum_fusion.refs_1_), custom_call_target="tpu_custom_call" | custom-call | bytes 5898240 | tf_op jit(solution)/shard_map/pallas_call | solution.py:146
  579.8 8.6 %shard_map.311 = (bf16[512,256]{1,0:T(8,128)(2,1)S(1)}, bf16[1536,512]{1,0:T(8,128)(2,1)S(1)}) custom-call(bf16[2,4,256,1280]{3,2,1,0:T(8,128)(2,1)} %get-tuple-element.117.weights_ref, bf16[512,384]{1,0:T(8,128)(2,1)S(1)} %convolution_convert_fusion.5.grad_ref, bf16[512,384]{1,0:T(8,128)(2,1)S(1)} %fusion.28.q_ref, bf16[1536,768]{1,0:T(8,128)(2,1)S(1)} %add_convert_fusion.kv_ref), custom_call_target="tpu_custom_call" | custom-call | flops 5368709120 | bytes 10485760 | tf_op jit(solution)/shard_map/pallas_call | solution.py:342
  590.1 10.6 %collective-permute-done.34 = bf16[4,96,384]{2,1,0:T(8,128)(2,1)S(1)} collective-permute-done((bf16[4,96,384]{2,1,0:T(8,128)(2,1)}, bf16[4,96,384]{2,1,0:T(8,128)(2,1)S(1)}, u32[]{:S(2)}, u32[]{:S(2)}) %collective-permute-start.34) | collective-permute-done | bytes 294944 | tf_op jit(solution)/shard_map/ppermute | solution.py:78
  601.5 2.6 collective-permute-start.54
  605.9 4.9 shard_map.312
  611.1 4.2 collective-permute-done.55
  615.3 2.6 collective-permute-done.56
  625.5 3.2 convolution_convert_fusion.2
  631.7 2.8 fusion.48
  636.2 7.0 fusion.84
  645.9 2.9 fusion.27.refs_1_
  648.8 61.0 %shard_map.314 = (bf16[8,48,640]{2,1,0:T(8,128)(2,1)}, bf16[8,48,640]{2,1,0:T(8,128)(2,1)}, bf16[8,48,640]{2,1,0:T(8,128)(2,1)}, bf16[8,48,640]{2,1,0:T(8,128)(2,1)}) custom-call(s32[1]{0:T(128)} %bitcast.16.refs_0_, bf16[768,1280]{1,0:T(8,128)(2,1)} %fusion.27.refs_1_), custom_call_target="tpu_custom_call" | custom-call | bytes 3932160 | tf_op jit(solution)/shard_map/pallas_call | solution.py:146
  712.1 2.6 fusion.29
  716.3 13.6 %collective-permute-done.49 = bf16[4,48,1024]{2,1,0:T(8,128)(2,1)S(1)} collective-permute-done((bf16[4,48,1024]{2,1,0:T(8,128)(2,1)}, bf16[4,48,1024]{2,1,0:T(8,128)(2,1)S(1)}, u32[]{:S(2)}, u32[]{:S(2)}) %collective-permute-start.49) | collective-permute-done | bytes 393248 | tf_op jit(solution)/shard_map/ppermute | solution.py:78
  730.2 2.6 collective-permute-start.51
  734.4 3.3 collective-permute-done.50
  738.9 4.5 collective-permute-done.51
  743.3 3.8 collective-permute-done.52
  757.7 2.5 collective-permute-done.45
  760.2 3.7 collective-permute-done.46
  768.3 3.2 fusion.93
  772.3 3.1 collective-permute-start.38
  778.4 7.6 collective-permute-done.38
  786.0 13.8 %collective-permute-done.39 = bf16[256,768]{1,0:T(8,128)(2,1)} collective-permute-done((bf16[256,768]{1,0:T(8,128)(2,1)S(1)}, bf16[256,768]{1,0:T(8,128)(2,1)}, u32[]{:S(2)}, u32[]{:S(2)}) %collective-permute-start.39) | collective-permute-done | bytes 393248 | tf_op jit(solution)/shard_map/ppermute | solution.py:74
  (425 shorter events, 149.2 us)
Async XLA Ops:
  0.7 14.7 %collective-permute-start.5 = (bf16[256,768]{1,0:T(8,128)(2,1)}, bf16[256,768]{1,0:T(8,128)(2,1)S(1)}, u32[]{:S(2)}, u32[]{:S(2)}) collective-permute-start(bf16[256,768]{1,0:T(8,128)(2,1)} %param.18), channel_id=1, source_target_pairs={{0,2},{1,3},{2,4},{3,5},{4,6},{5,7},{6,8},{7,9},{8,10},{9,11},{10,... | collective-permute-start | bytes 1179656 | tf_op jit(solution)/shard_map/ppermute | solution.py:74
  4.2 18.9 %collective-permute-start.4 = (bf16[256,768]{1,0:T(8,128)(2,1)}, bf16[256,768]{1,0:T(8,128)(2,1)S(1)}, u32[]{:S(2)}, u32[]{:S(2)}) collective-permute-start(bf16[256,768]{1,0:T(8,128)(2,1)} %param.18), channel_id=1, source_target_pairs={{0,4},{1,5},{2,6},{3,7},{4,8},{5,9},{6,10},{7,11},{8,12},{9,13},{1... | collective-permute-start | bytes 1179656 | tf_op jit(solution)/shard_map/ppermute | solution.py:74
  13.5 9.8 %collective-permute-start = (bf16[24,3200]{1,0:T(8,128)(2,1)S(1)}, bf16[24,3200]{1,0:T(8,128)(2,1)S(1)}, u32[]{:S(2)}, u32[]{:S(2)}) collective-permute-start(bf16[24,3200]{1,0:T(8,128)(2,1)S(1)} %broadcast_select_fusion.9), channel_id=1, source_target_pairs={{0,1},{1,0},{2,3},{3,2},{4,5},{5,4},{6,7},{7,6},{8,9},{9,8},{10,11... | collective-permute-start | bytes 460808 | tf_op jit(solution)/shard_map/ppermute | solution.py:78
  14.1 24.3 %collective-permute-start.15 = (bf16[256,768]{1,0:T(8,128)(2,1)S(1)}, bf16[256,768]{1,0:T(8,128)(2,1)}, u32[]{:S(2)}, u32[]{:S(2)}) collective-permute-start(bf16[256,768]{1,0:T(8,128)(2,1)S(1)} %copy-done.22), channel_id=1, source_target_pairs={{0,1},{1,0},{2,3},{3,2},{4,5},{5,4},{6,7},{7,6},{8,9},{9,8},{10,11... | collective-permute-start | bytes 1179656 | tf_op jit(solution)/shard_map/ppermute | solution.py:78
  23.2 17.1 %collective-permute-start.6 = (bf16[3,256,768]{2,1,0:T(8,128)(2,1)S(1)}, bf16[3,256,768]{2,1,0:T(8,128)(2,1)S(1)}, u32[]{:S(2)}, u32[]{:S(2)}) collective-permute-start(bf16[3,256,768]{2,1,0:T(8,128)(2,1)S(1)} %pad_maximum_fusion.5), channel_id=1, source_target_pairs={{0,1},{1,0},{2,3},{3,2},{4,5},{5,4},{6,7},{7,6},{8,9},{9,8},{10,11... | collective-permute-start | bytes 3538952 | tf_op jit(solution)/shard_map/ppermute | solution.py:78
  23.9 11.6 %collective-permute-start.2 = (bf16[48,1280]{1,0:T(8,128)(2,1)S(1)}, bf16[48,1280]{1,0:T(8,128)(2,1)S(1)}, u32[]{:S(2)}, u32[]{:S(2)}) collective-permute-start(bf16[48,1280]{1,0:T(8,128)(2,1)S(1)} %pad_maximum_fusion.29), channel_id=1, source_target_pairs={{0,16},{1,17},{2,18},{3,19},{4,20},{5,21},{6,22},{7,23},{8,24},{9,... | collective-permute-start | bytes 368648 | tf_op jit(solution)/shard_map/ppermute | solution.py:78
  26.5 11.8 %collective-permute-start.3 = (bf16[48,1280]{1,0:T(8,128)(2,1)S(1)}, bf16[48,1280]{1,0:T(8,128)(2,1)S(1)}, u32[]{:S(2)}, u32[]{:S(2)}) collective-permute-start(bf16[48,1280]{1,0:T(8,128)(2,1)S(1)} %pad_maximum_fusion.29), channel_id=1, source_target_pairs={{0,24},{1,25},{2,26},{3,27},{4,28},{5,29},{6,30},{7,31},{8,16},{9,... | collective-permute-start | bytes 368648 | tf_op jit(solution)/shard_map/ppermute | solution.py:78
  41.0 17.8 %collective-permute-start.12 = (bf16[48,1920]{1,0:T(8,128)(2,1)S(1)}, bf16[48,1920]{1,0:T(8,128)(2,1)}, u32[]{:S(2)}, u32[]{:S(2)}) collective-permute-start(bf16[48,1920]{1,0:T(8,128)(2,1)S(1)} %pad_maximum_fusion.22), channel_id=1, source_target_pairs={{0,8},{1,9},{2,10},{3,11},{4,12},{5,13},{6,14},{7,15},{8,0},{9,1},... | collective-permute-start | bytes 552968 | tf_op jit(solution)/shard_map/ppermute | solution.py:78
  41.1 17.7 %collective-permute-start.13 = (bf16[48,1920]{1,0:T(8,128)(2,1)S(1)}, bf16[48,1920]{1,0:T(8,128)(2,1)}, u32[]{:S(2)}, u32[]{:S(2)}) collective-permute-start(bf16[48,1920]{1,0:T(8,128)(2,1)S(1)} %pad_maximum_fusion.22), channel_id=1, source_target_pairs={{0,16},{1,17},{2,18},{3,19},{4,20},{5,21},{6,22},{7,23},{8,24},{9,... | collective-permute-start | bytes 552968 | tf_op jit(solution)/shard_map/ppermute | solution.py:78
  44.1 16.1 %collective-permute-start.14 = (bf16[48,1920]{1,0:T(8,128)(2,1)S(1)}, bf16[48,1920]{1,0:T(8,128)(2,1)}, u32[]{:S(2)}, u32[]{:S(2)}) collective-permute-start(bf16[48,1920]{1,0:T(8,128)(2,1)S(1)} %pad_maximum_fusion.22), channel_id=1, source_target_pairs={{0,24},{1,25},{2,26},{3,27},{4,28},{5,29},{6,30},{7,31},{8,16},{9,... | collective-permute-start | bytes 552968 | tf_op jit(solution)/shard_map/ppermute | solution.py:78
  52.5 12.0 %collective-permute-start.11 = (bf16[8,48,640]{2,1,0:T(8,128)(2,1)}, bf16[8,48,640]{2,1,0:T(8,128)(2,1)}, u32[]{:S(2)}, u32[]{:S(2)}) collective-permute-start(bf16[8,48,640]{2,1,0:T(8,128)(2,1)} %pad_maximum_fusion.18.refs_3_), channel_id=1, source_target_pairs={{0,4},{1,5},{2,6},{3,7},{4,0},{5,1},{6,2},{7,3},{8,12},{9,13},{10,... | collective-permute-start | bytes 1474568 | tf_op jit(solution)/shard_map/ppermute | solution.py:78
  55.6 11.2 %collective-permute-start.9 = (bf16[8,48,640]{2,1,0:T(8,128)(2,1)}, bf16[8,48,640]{2,1,0:T(8,128)(2,1)}, u32[]{:S(2)}, u32[]{:S(2)}) collective-permute-start(bf16[8,48,640]{2,1,0:T(8,128)(2,1)} %pad_maximum_fusion.17.refs_1_), channel_id=1, source_target_pairs={{0,2},{1,3},{2,0},{3,1},{4,6},{5,7},{6,4},{7,5},{8,10},{9,11},{10,... | collective-permute-start | bytes 1474568 | tf_op jit(solution)/shard_map/ppermute | solution.py:78
  66.7 78.9 %collective-permute-start.18 = (bf16[96,768]{1,0:T(8,128)(2,1)S(1)}, bf16[96,768]{1,0:T(8,128)(2,1)}, u32[]{:S(2)}, u32[]{:S(2)}) collective-permute-start(bf16[96,768]{1,0:T(8,128)(2,1)S(1)} %reshape.265), channel_id=1, source_target_pairs={{0,8},{1,9},{2,10},{3,11},{4,12},{5,13},{6,14},{7,15},{8,0},{9,1},... | collective-permute-start | bytes 442376 | tf_op jit(solution)/shard_map/ppermute | solution.py:78
  68.3 77.4 %collective-permute-start.19 = (bf16[96,768]{1,0:T(8,128)(2,1)S(1)}, bf16[96,768]{1,0:T(8,128)(2,1)}, u32[]{:S(2)}, u32[]{:S(2)}) collective-permute-start(bf16[96,768]{1,0:T(8,128)(2,1)S(1)} %reshape.265), channel_id=1, source_target_pairs={{0,16},{1,17},{2,18},{3,19},{4,20},{5,21},{6,22},{7,23},{8,24},{9,... | collective-permute-start | bytes 442376 | tf_op jit(solution)/shard_map/ppermute | solution.py:78
  69.8 75.9 %collective-permute-start.20 = (bf16[96,768]{1,0:T(8,128)(2,1)S(1)}, bf16[96,768]{1,0:T(8,128)(2,1)}, u32[]{:S(2)}, u32[]{:S(2)}) collective-permute-start(bf16[96,768]{1,0:T(8,128)(2,1)S(1)} %reshape.265), channel_id=1, source_target_pairs={{0,24},{1,25},{2,26},{3,27},{4,28},{5,29},{6,30},{7,31},{8,16},{9,... | collective-permute-start | bytes 442376 | tf_op jit(solution)/shard_map/ppermute | solution.py:78
  71.8 76.2 %collective-permute-start.17 = (bf16[4,48,1024]{2,1,0:T(8,128)(2,1)}, bf16[4,48,1024]{2,1,0:T(8,128)(2,1)}, u32[]{:S(2)}, u32[]{:S(2)}) collective-permute-start(bf16[4,48,1024]{2,1,0:T(8,128)(2,1)} %slice.442), channel_id=1, source_target_pairs={{0,2},{1,3},{2,0},{3,1},{4,6},{5,7},{6,4},{7,5},{8,10},{9,11},{10,... | collective-permute-start | bytes 1179656 | tf_op jit(solution)/shard_map/ppermute | solution.py:78
  73.3 73.6 %collective-permute-start.16 = (bf16[4,48,896]{2,1,0:T(8,128)(2,1)}, bf16[4,48,896]{2,1,0:T(8,128)(2,1)}, u32[]{:S(2)}, u32[]{:S(2)}) collective-permute-start(bf16[4,48,896]{2,1,0:T(8,128)(2,1)} %slice.441), channel_id=1, source_target_pairs={{0,4},{1,5},{2,6},{3,7},{4,0},{5,1},{6,2},{7,3},{8,12},{9,13},{10,... | collective-permute-start | bytes 1032200 | tf_op jit(solution)/shard_map/ppermute | solution.py:78
  158.6 22.3 %collective-permute-start.22 = (bf16[8,48,1024]{2,1,0:T(8,128)(2,1)S(1)}, bf16[8,48,1024]{2,1,0:T(8,128)(2,1)S(1)}, u32[]{:S(2)}, u32[]{:S(2)}) collective-permute-start(bf16[8,48,1024]{2,1,0:T(8,128)(2,1)S(1)} %pad_maximum_fusion.7.refs_3_), channel_id=1, source_target_pairs={{0,4},{1,5},{2,6},{3,7},{4,0},{5,1},{6,2},{7,3},{8,12},{9,13},{10,... | collective-permute-start | bytes 2359304 | tf_op jit(solution)/shard_map/ppermute | solution.py:78
  160.5 10.0 %collective-permute-start.24 = (bf16[4,96,384]{2,1,0:T(8,128)(2,1)S(1)}, bf16[4,96,384]{2,1,0:T(8,128)(2,1)S(1)}, u32[]{:S(2)}, u32[]{:S(2)}) collective-permute-start(bf16[4,96,384]{2,1,0:T(8,128)(2,1)S(1)} %get-tuple-element.238), channel_id=1, source_target_pairs={{0,2},{1,3},{2,0},{3,1},{4,6},{5,7},{6,4},{7,5},{8,10},{9,11},{10,... | collective-permute-start | bytes 884744 | tf_op jit(solution)/shard_map/ppermute | solution.py:78
  161.1 19.8 %collective-permute-start.21 = (bf16[8,48,896]{2,1,0:T(8,128)(2,1)S(1)}, bf16[8,48,896]{2,1,0:T(8,128)(2,1)S(1)}, u32[]{:S(2)}, u32[]{:S(2)}) collective-permute-start(bf16[8,48,896]{2,1,0:T(8,128)(2,1)S(1)} %pad_maximum_fusion.10.refs_1_), channel_id=1, source_target_pairs={{0,2},{1,3},{2,0},{3,1},{4,6},{5,7},{6,4},{7,5},{8,10},{9,11},{10,... | collective-permute-start | bytes 2064392 | tf_op jit(solution)/shard_map/ppermute | solution.py:78
  163.2 16.8 %collective-permute-start.23 = (bf16[4,96,384]{2,1,0:T(8,128)(2,1)S(1)}, bf16[4,96,384]{2,1,0:T(8,128)(2,1)S(1)}, u32[]{:S(2)}, u32[]{:S(2)}) collective-permute-start(bf16[4,96,384]{2,1,0:T(8,128)(2,1)S(1)} %get-tuple-element.239), channel_id=1, source_target_pairs={{0,4},{1,5},{2,6},{3,7},{4,0},{5,1},{6,2},{7,3},{8,12},{9,13},{10,... | collective-permute-start | bytes 884744 | tf_op jit(solution)/shard_map/ppermute | solution.py:78
  181.9 101.2 %collective-permute-start.25 = (bf16[512,384]{1,0:T(8,128)(2,1)S(1)}, bf16[512,384]{1,0:T(8,128)(2,1)}, u32[]{:S(2)}, u32[]{:S(2)}) collective-permute-start(bf16[512,384]{1,0:T(8,128)(2,1)S(1)} %pad_maximum_fusion.19), channel_id=1, source_target_pairs={{0,1},{1,0},{2,3},{3,2},{4,5},{5,4},{6,7},{7,6},{8,9},{9,8},{10,11... | collective-permute-start | bytes 1179656 | tf_op jit(solution)/shard_map/ppermute | solution.py:78
  280.8 88.0 %collective-permute-start.27 = (bf16[8,96,384]{2,1,0:T(8,128)(2,1)}, bf16[8,96,384]{2,1,0:T(8,128)(2,1)}, u32[]{:S(2)}, u32[]{:S(2)}) collective-permute-start(bf16[8,96,384]{2,1,0:T(8,128)(2,1)} %pad_maximum_fusion.12.refs_1_), channel_id=1, source_target_pairs={{0,2},{1,3},{2,0},{3,1},{4,6},{5,7},{6,4},{7,5},{8,10},{9,11},{10,... | collective-permute-start | bytes 1769480 | tf_op jit(solution)/shard_map/ppermute | solution.py:78
  281.4 87.4 %collective-permute-start.28 = (bf16[8,96,384]{2,1,0:T(8,128)(2,1)}, bf16[8,96,384]{2,1,0:T(8,128)(2,1)}, u32[]{:S(2)}, u32[]{:S(2)}) collective-permute-start(bf16[8,96,384]{2,1,0:T(8,128)(2,1)} %pad_maximum_fusion.13.refs_3_), channel_id=1, source_target_pairs={{0,4},{1,5},{2,6},{3,7},{4,0},{5,1},{6,2},{7,3},{8,12},{9,13},{10,... | collective-permute-start | bytes 1769480 | tf_op jit(solution)/shard_map/ppermute | solution.py:78
  368.5 95.9 %collective-permute-start.32 = (bf16[8,96,384]{2,1,0:T(8,128)(2,1)}, bf16[8,96,384]{2,1,0:T(8,128)(2,1)}, u32[]{:S(2)}, u32[]{:S(2)}) collective-permute-start(bf16[8,96,384]{2,1,0:T(8,128)(2,1)} %get-tuple-element.122), channel_id=1, source_target_pairs={{0,4},{1,5},{2,6},{3,7},{4,0},{5,1},{6,2},{7,3},{8,12},{9,13},{10,... | collective-permute-start | bytes 1769480 | tf_op jit(solution)/shard_map/ppermute | solution.py:78
  457.2 16.0 %collective-permute-start.31 = (bf16[8,96,384]{2,1,0:T(8,128)(2,1)}, bf16[8,96,384]{2,1,0:T(8,128)(2,1)}, u32[]{:S(2)}, u32[]{:S(2)}) collective-permute-start(bf16[8,96,384]{2,1,0:T(8,128)(2,1)} %get-tuple-element.120), channel_id=1, source_target_pairs={{0,2},{1,3},{2,0},{3,1},{4,6},{5,7},{6,4},{7,5},{8,10},{9,11},{10,... | collective-permute-start | bytes 1769480 | tf_op jit(solution)/shard_map/ppermute | solution.py:78
  458.6 16.6 %collective-permute-start.30 = (bf16[512,768]{1,0:T(8,128)(2,1)}, bf16[512,768]{1,0:T(8,128)(2,1)}, u32[]{:S(2)}, u32[]{:S(2)}) collective-permute-start(bf16[512,768]{1,0:T(8,128)(2,1)} %get-tuple-element.284), channel_id=1, source_target_pairs={{0,1},{1,0},{2,3},{3,2},{4,5},{5,4},{6,7},{7,6},{8,9},{9,8},{10,11... | collective-permute-start | bytes 2359304 | tf_op jit(solution)/shard_map/ppermute | solution.py:78
  575.7 47.6 %collective-permute-start.36 = (bf16[8,48,1024]{2,1,0:T(8,128)(2,1)}, bf16[8,48,1024]{2,1,0:T(8,128)(2,1)}, u32[]{:S(2)}, u32[]{:S(2)}) collective-permute-start(bf16[8,48,1024]{2,1,0:T(8,128)(2,1)} %get-tuple-element.140), channel_id=1, source_target_pairs={{0,4},{1,5},{2,6},{3,7},{4,0},{5,1},{6,2},{7,3},{8,12},{9,13},{10,... | collective-permute-start | bytes 2359304 | tf_op jit(solution)/shard_map/ppermute | solution.py:78
  577.5 43.5 %collective-permute-start.35 = (bf16[8,48,896]{2,1,0:T(8,128)(2,1)}, bf16[8,48,896]{2,1,0:T(8,128)(2,1)}, u32[]{:S(2)}, u32[]{:S(2)}) collective-permute-start(bf16[8,48,896]{2,1,0:T(8,128)(2,1)} %get-tuple-element.138), channel_id=1, source_target_pairs={{0,2},{1,3},{2,0},{3,1},{4,6},{5,7},{6,4},{7,5},{8,10},{9,11},{10,... | collective-permute-start | bytes 2064392 | tf_op jit(solution)/shard_map/ppermute | solution.py:78
  578.7 22.1 %collective-permute-start.34 = (bf16[4,96,384]{2,1,0:T(8,128)(2,1)}, bf16[4,96,384]{2,1,0:T(8,128)(2,1)S(1)}, u32[]{:S(2)}, u32[]{:S(2)}) collective-permute-start(bf16[4,96,384]{2,1,0:T(8,128)(2,1)} %get-tuple-element.129), channel_id=1, source_target_pairs={{0,2},{1,3},{2,0},{3,1},{4,6},{5,7},{6,4},{7,5},{8,10},{9,11},{10,... | collective-permute-start | bytes 884744 | tf_op jit(solution)/shard_map/ppermute | solution.py:78
  579.5 21.9 %collective-permute-start.33 = (bf16[4,96,384]{2,1,0:T(8,128)(2,1)}, bf16[4,96,384]{2,1,0:T(8,128)(2,1)S(1)}, u32[]{:S(2)}, u32[]{:S(2)}) collective-permute-start(bf16[4,96,384]{2,1,0:T(8,128)(2,1)} %get-tuple-element.127), channel_id=1, source_target_pairs={{0,4},{1,5},{2,6},{3,7},{4,0},{5,1},{6,2},{7,3},{8,12},{9,13},{10,... | collective-permute-start | bytes 884744 | tf_op jit(solution)/shard_map/ppermute | solution.py:78
  601.5 9.5 %collective-permute-start.54 = (bf16[96,768]{1,0:T(8,128)(2,1)S(1)}, bf16[96,768]{1,0:T(8,128)(2,1)S(1)}, u32[]{:S(2)}, u32[]{:S(2)}) collective-permute-start(bf16[96,768]{1,0:T(8,128)(2,1)S(1)} %pad_maximum_fusion.26), channel_id=1, source_target_pairs={{0,8},{1,9},{2,10},{3,11},{4,12},{5,13},{6,14},{7,15},{8,0},{9,1},... | collective-permute-start | bytes 442376 | tf_op jit(solution)/shard_map/ppermute | solution.py:78
  604.2 11.1 %collective-permute-start.55 = (bf16[96,768]{1,0:T(8,128)(2,1)S(1)}, bf16[96,768]{1,0:T(8,128)(2,1)S(1)}, u32[]{:S(2)}, u32[]{:S(2)}) collective-permute-start(bf16[96,768]{1,0:T(8,128)(2,1)S(1)} %pad_maximum_fusion.27), channel_id=1, source_target_pairs={{0,16},{1,17},{2,18},{3,19},{4,20},{5,21},{6,22},{7,23},{8,24},{9,... | collective-permute-start | bytes 442376 | tf_op jit(solution)/shard_map/ppermute | solution.py:78
  605.3 12.6 %collective-permute-start.56 = (bf16[96,768]{1,0:T(8,128)(2,1)S(1)}, bf16[96,768]{1,0:T(8,128)(2,1)S(1)}, u32[]{:S(2)}, u32[]{:S(2)}) collective-permute-start(bf16[96,768]{1,0:T(8,128)(2,1)S(1)} %pad_maximum_fusion.28), channel_id=1, source_target_pairs={{0,24},{1,25},{2,26},{3,27},{4,28},{5,29},{6,30},{7,31},{8,16},{9,... | collective-permute-start | bytes 442376 | tf_op jit(solution)/shard_map/ppermute | solution.py:78
  644.1 70.7 %collective-permute-start.48 = (bf16[4,48,896]{2,1,0:T(8,128)(2,1)}, bf16[4,48,896]{2,1,0:T(8,128)(2,1)}, u32[]{:S(2)}, u32[]{:S(2)}) collective-permute-start(bf16[4,48,896]{2,1,0:T(8,128)(2,1)} %get-tuple-element.148), channel_id=1, source_target_pairs={{0,4},{1,5},{2,6},{3,7},{4,0},{5,1},{6,2},{7,3},{8,12},{9,13},{10,... | collective-permute-start | bytes 1032200 | tf_op jit(solution)/shard_map/ppermute | solution.py:78
  709.8 23.0 %collective-permute-start.40 = (bf16[8,48,640]{2,1,0:T(8,128)(2,1)}, bf16[8,48,640]{2,1,0:T(8,128)(2,1)S(1)}, u32[]{:S(2)}, u32[]{:S(2)}) collective-permute-start(bf16[8,48,640]{2,1,0:T(8,128)(2,1)} %get-tuple-element.144), channel_id=1, source_target_pairs={{0,2},{1,3},{2,0},{3,1},{4,6},{5,7},{6,4},{7,5},{8,10},{9,11},{10,... | collective-permute-start | bytes 1474568 | tf_op jit(solution)/shard_map/ppermute | solution.py:78
  711.0 22.9 %collective-permute-start.42 = (bf16[8,48,640]{2,1,0:T(8,128)(2,1)}, bf16[8,48,640]{2,1,0:T(8,128)(2,1)S(1)}, u32[]{:S(2)}, u32[]{:S(2)}) collective-permute-start(bf16[8,48,640]{2,1,0:T(8,128)(2,1)} %get-tuple-element.146), channel_id=1, source_target_pairs={{0,4},{1,5},{2,6},{3,7},{4,0},{5,1},{6,2},{7,3},{8,12},{9,13},{10,... | collective-permute-start | bytes 1474568 | tf_op jit(solution)/shard_map/ppermute | solution.py:78
  711.6 18.3 %collective-permute-start.49 = (bf16[4,48,1024]{2,1,0:T(8,128)(2,1)}, bf16[4,48,1024]{2,1,0:T(8,128)(2,1)S(1)}, u32[]{:S(2)}, u32[]{:S(2)}) collective-permute-start(bf16[4,48,1024]{2,1,0:T(8,128)(2,1)} %get-tuple-element.150), channel_id=1, source_target_pairs={{0,2},{1,3},{2,0},{3,1},{4,6},{5,7},{6,4},{7,5},{8,10},{9,11},{10,... | collective-permute-start | bytes 1179656 | tf_op jit(solution)/shard_map/ppermute | solution.py:78
  714.8 53.6 %collective-permute-start.37 = (bf16[3,256,768]{2,1,0:T(8,128)(2,1)S(1)}, bf16[3,256,768]{2,1,0:T(8,128)(2,1)}, u32[]{:S(2)}, u32[]{:S(2)}) collective-permute-start(bf16[3,256,768]{2,1,0:T(8,128)(2,1)S(1)} %fusion.29), channel_id=1, source_target_pairs={{0,1},{1,0},{2,3},{3,2},{4,5},{5,4},{6,7},{7,6},{8,9},{9,8},{10,11... | collective-permute-start | bytes 3538952 | tf_op jit(solution)/shard_map/ppermute | solution.py:78
  730.2 13.2 %collective-permute-start.51 = (bf16[48,1920]{1,0:T(8,128)(2,1)S(1)}, bf16[48,1920]{1,0:T(8,128)(2,1)S(1)}, u32[]{:S(2)}, u32[]{:S(2)}) collective-permute-start(bf16[48,1920]{1,0:T(8,128)(2,1)S(1)} %pad_maximum_fusion.24), channel_id=1, source_target_pairs={{0,16},{1,17},{2,18},{3,19},{4,20},{5,21},{6,22},{7,23},{8,24},{9,... | collective-permute-start | bytes 552968 | tf_op jit(solution)/shard_map/ppermute | solution.py:78
  732.7 14.4 %collective-permute-start.52 = (bf16[48,1920]{1,0:T(8,128)(2,1)S(1)}, bf16[48,1920]{1,0:T(8,128)(2,1)S(1)}, u32[]{:S(2)}, u32[]{:S(2)}) collective-permute-start(bf16[48,1920]{1,0:T(8,128)(2,1)S(1)} %pad_maximum_fusion.25), channel_id=1, source_target_pairs={{0,24},{1,25},{2,26},{3,27},{4,28},{5,29},{6,30},{7,31},{8,16},{9,... | collective-permute-start | bytes 552968 | tf_op jit(solution)/shard_map/ppermute | solution.py:78
  733.9 13.4 %collective-permute-start.41 = (bf16[4,48,640]{2,1,0:T(8,128)(2,1)S(1)}, bf16[4,48,640]{2,1,0:T(8,128)(2,1)S(1)}, u32[]{:S(2)}, u32[]{:S(2)}) collective-permute-start(bf16[4,48,640]{2,1,0:T(8,128)(2,1)S(1)} %get-tuple-element.215), channel_id=1, source_target_pairs={{0,4},{1,5},{2,6},{3,7},{4,0},{5,1},{6,2},{7,3},{8,12},{9,13},{10,... | collective-permute-start | bytes 737288 | tf_op jit(solution)/shard_map/ppermute | solution.py:78
  737.7 9.8 %collective-permute-start.43 = (bf16[4,48,640]{2,1,0:T(8,128)(2,1)S(1)}, bf16[4,48,640]{2,1,0:T(8,128)(2,1)S(1)}, u32[]{:S(2)}, u32[]{:S(2)}) collective-permute-start(bf16[4,48,640]{2,1,0:T(8,128)(2,1)S(1)} %get-tuple-element.217), channel_id=1, source_target_pairs={{0,2},{1,3},{2,0},{3,1},{4,6},{5,7},{6,4},{7,5},{8,10},{9,11},{10,... | collective-permute-start | bytes 737288 | tf_op jit(solution)/shard_map/ppermute | solution.py:78
  748.2 9.5 %collective-permute-start.44 = (bf16[48,1280]{1,0:T(8,128)(2,1)}, bf16[48,1280]{1,0:T(8,128)(2,1)}, u32[]{:S(2)}, u32[]{:S(2)}) collective-permute-start(bf16[48,1280]{1,0:T(8,128)(2,1)} %pad_maximum_fusion.30), channel_id=1, source_target_pairs={{0,8},{1,9},{2,10},{3,11},{4,12},{5,13},{6,14},{7,15},{8,0},{9,1},... | collective-permute-start | bytes 368648 | tf_op jit(solution)/shard_map/ppermute | solution.py:78
  748.9 11.4 %collective-permute-start.45 = (bf16[48,1280]{1,0:T(8,128)(2,1)}, bf16[48,1280]{1,0:T(8,128)(2,1)}, u32[]{:S(2)}, u32[]{:S(2)}) collective-permute-start(bf16[48,1280]{1,0:T(8,128)(2,1)} %pad_maximum_fusion.31), channel_id=1, source_target_pairs={{0,16},{1,17},{2,18},{3,19},{4,20},{5,21},{6,22},{7,23},{8,24},{9,... | collective-permute-start | bytes 368648 | tf_op jit(solution)/shard_map/ppermute | solution.py:78
  751.6 12.3 %collective-permute-start.46 = (bf16[48,1280]{1,0:T(8,128)(2,1)}, bf16[48,1280]{1,0:T(8,128)(2,1)}, u32[]{:S(2)}, u32[]{:S(2)}) collective-permute-start(bf16[48,1280]{1,0:T(8,128)(2,1)} %pad_maximum_fusion.32), channel_id=1, source_target_pairs={{0,24},{1,25},{2,26},{3,27},{4,28},{5,29},{6,30},{7,31},{8,16},{9,... | collective-permute-start | bytes 368648 | tf_op jit(solution)/shard_map/ppermute | solution.py:78
  772.3 13.7 %collective-permute-start.38 = (bf16[256,768]{1,0:T(8,128)(2,1)}, bf16[256,768]{1,0:T(8,128)(2,1)}, u32[]{:S(2)}, u32[]{:S(2)}) collective-permute-start(bf16[256,768]{1,0:T(8,128)(2,1)} %get-tuple-element.208), channel_id=1, source_target_pairs={{2,0},{3,1},{4,2},{5,3},{6,4},{7,5},{8,6},{9,7},{10,8},{11,9},{12,... | collective-permute-start | bytes 1179656 | tf_op jit(solution)/shard_map/ppermute | solution.py:74
  775.4 24.4 %collective-permute-start.39 = (bf16[256,768]{1,0:T(8,128)(2,1)S(1)}, bf16[256,768]{1,0:T(8,128)(2,1)}, u32[]{:S(2)}, u32[]{:S(2)}) collective-permute-start(bf16[256,768]{1,0:T(8,128)(2,1)S(1)} %get-tuple-element.209), channel_id=1, source_target_pairs={{4,0},{5,1},{6,2},{7,3},{8,4},{9,5},{10,6},{11,7},{12,8},{13,9},{1... | collective-permute-start | bytes 1179656 | tf_op jit(solution)/shard_map/ppermute | solution.py:74
  (86 other events, 1002.8 us)
